TPU v7x, 32 devices: a whole 2x2x4 slice. The times are simulated.
32 devices in a mesh: fsdp: 8 (over y, x, core), ns: 4 (over z).
Axes of the slice: x: 2, y: 2, z: 4, core: 2. Of those that a mesh axis runs over, the one named last changes fastest.
Arguments:
- tokens: bfloat16 [32, 256, 1024], P(('fsdp', 'ns')), may hold values from -6 to 6
- out_grad: bfloat16 [32, 256, 1024], P(('fsdp', 'ns')), may hold values from -6 to 6
- doc_lengths: int32 [32, 4], P(('fsdp', 'ns')), may hold values from 1 to 128, 256 in all within a row
- in_proj: float32 [4096, 1024], P(('fsdp', 'ns')), may hold values from -0.1875 to 0.1875
- inner_projection_weight: float32 [2048, 96], P(('fsdp', 'ns')), may hold values from -0.125 to 0.125
- dt_proj: float32 [2048, 64], P(('fsdp', 'ns')), may hold values from -0.75 to 0.75
- out_proj: float32 [2048, 1024], P(('fsdp', 'ns')), may hold values from -0.375 to 0.375
- in_moment: float32 [4096, 1024], P(('fsdp', 'ns')), may hold values from -162.9174 to 162.9174
- x_moment: float32 [2048, 96], P(('fsdp', 'ns')), may hold values from -244.3761 to 244.3761
- dt_moment: float32 [2048, 64], P(('fsdp', 'ns')), may hold values from -244.3761 to 244.3761
- out_moment: float32 [2048, 1024], P(('fsdp', 'ns')), may hold values from -244.3761 to 244.3761
- vectors: float32 [23, 2048], P(None, ('fsdp', 'ns')), may hold values from -7 to 3, as said below
- vector_first: float32 [23, 2048], P(None, ('fsdp', 'ns')), may hold values from -9.050967 to 9.050967
- vector_second: float32 [23, 2048], P(None, ('fsdp', 'ns')), may hold values from 0.016384 to 327.68
- norm_gain: float32 [1024], P(('fsdp', 'ns')), may hold values from 0.5 to 1.5
- gain_first: float32 [1024], P(('fsdp', 'ns')), may hold values from -16 to 16
- gain_second: float32 [1024], P(('fsdp', 'ns')), may hold values from 19.6608 to 311.296
Outputs:
- block_out: float32 [32, 256, 1024], P(('fsdp', 'ns'))
- grad_tokens: float32 [32, 256, 1024], P(('fsdp', 'ns'))
- in_proj_new: float32 [4096, 1024], P(('fsdp', 'ns'))
- in_moment_new: float32 [4096, 1024], P(('fsdp', 'ns'))
- x_proj_new: float32 [2048, 96], P(('fsdp', 'ns'))
- x_moment_new: float32 [2048, 96], P(('fsdp', 'ns'))
- dt_proj_new: float32 [2048, 64], P(('fsdp', 'ns'))
- dt_moment_new: float32 [2048, 64], P(('fsdp', 'ns'))
- out_proj_new: float32 [2048, 1024], P(('fsdp', 'ns'))
- out_moment_new: float32 [2048, 1024], P(('fsdp', 'ns'))
- vectors_new: float32 [23, 2048], P(None, ('fsdp', 'ns'))
- vector_first_new: float32 [23, 2048], P(None, ('fsdp', 'ns'))
- vector_second_new: float32 [23, 2048], P(None, ('fsdp', 'ns'))
- norm_gain_new: float32 [1024], P(('fsdp', 'ns'))
- gain_first_new: float32 [1024], P(('fsdp', 'ns'))
- gain_second_new: float32 [1024], P(('fsdp', 'ns'))
Inputs may be any that keep to these rules, and one draw needn't show every extreme that they name: `doc_lengths`: each row's lengths add up to 256. `vectors`: a_log rows lie in 0 to log 16, skip gains in 0.5 to 1.5.
All inputs are finite; a program needn't handle non-finite values.
Results may differ from a plain program's by a relative error of at most 0.012.
Values may be sent and summed in bfloat16 or wider, within the bound.
A program may use at most 192 MiB of HBM per device.

v0:
```python
import math

import jax
import jax.numpy as jnp
from jax import lax
from jax.sharding import PartitionSpec as P

DMODEL = 1024
DINNER = 2048
DSTATE = 16
DTRANK = 64
KCONV = 4
BLOCK_LEN = 64
NS_STEPS = 4
STEP_NO = 10


NORM_EPS = 1e-05
FROB_EPS = 1e-07
COEF_A = 3.4445
COEF_B = -4.775
COEF_C = 2.0315
MOMENTUM = 0.95
SHRINK = 0.001
FIRST_MOMENT_BETA = 0.9
BETA_SECOND = 0.95
ADAM_EPS = 1e-08
ADAM_RATE = 1.0
ADAM_DECAY = 0.001


def as_sent(array):

    def short(part):
        return part.astype(jnp.bfloat16) if part.dtype == jnp.float32 else part

    return jax.tree.map(short, array)


def contract(left, right, left_dim, right_dim):
    return lax.dot_general(
        left, right, (((left_dim,), (right_dim,)), ((), ())), preferred_element_type=jnp.float32
    )


def segment_ids(lengths, length):
    ends = jnp.cumsum(lengths, axis=-1)
    starts = ends - lengths
    places = jnp.arange(length, dtype=jnp.int32)
    return jnp.sum(
        (places[None, :, None] >= starts[:, None, :]).astype(jnp.int32), axis=-1, dtype=jnp.int32
    )


def same_lag(segment, lag_index):
    length = segment.shape[1]
    earlier = jnp.pad(segment, ((0, 0), (lag_index, 0)), constant_values=-1)[:, :length]
    return (earlier == segment).astype(jnp.float32)


def lag_masks(segment):
    return [same_lag(segment, lag_index)[..., None] for lag_index in range(KCONV)]


def front_padded(value):
    return jnp.pad(value, ((0, 0), (KCONV - 1, 0), (0, 0)))


def lag_view(front, lag_index, length):
    begin = KCONV - 1 - lag_index
    return front[:, begin : begin + length]


def to_blocks(value, row_count, length):
    shaped = value.reshape((row_count, length // BLOCK_LEN, BLOCK_LEN) + value.shape[1:])
    return jnp.moveaxis(shaped, 1, 0)


def merge_from_blocks(value):
    merged = jnp.moveaxis(value, 0, 1)
    return merged.reshape((-1,) + merged.shape[3:])


def state_step(state, item):
    decay_t, drive_t = item
    state = decay_t * state + drive_t
    return (state, state)


def adjoint_step(adjoint, item):
    ahead_t, source_t = item
    adjoint = ahead_t * adjoint + source_t
    return (adjoint, adjoint)


def block_states(start, delta_b, b_block, u_block, keep_b, a_matrix):
    decay = jnp.exp(delta_b[:, :, None, :] * a_matrix) * keep_b[:, :, None, None]
    drive = (delta_b * u_block)[:, :, None, :] * b_block[:, :, :, None]
    unused, states = lax.scan(
        state_step, start, (jnp.moveaxis(decay, 1, 0), jnp.moveaxis(drive, 1, 0)), unroll=8
    )
    return (decay, jnp.moveaxis(states, 0, 1))


def scan_forward(delta, b_rows, c_rows, scan_input_value, keep, a_matrix, row_count, length):
    pieces = tuple(
        (
            to_blocks(value, row_count, length)
            for value in (delta, b_rows, c_rows, scan_input_value, keep)
        )
    )

    def advance(state, piece):
        delta_b, b_block, c_block, u_block, keep_b = piece
        unused, states = block_states(state, delta_b, b_block, u_block, keep_b, a_matrix)
        return (states[:, -1], (jnp.sum(states * c_block[:, :, :, None], axis=2), state))

    start = jnp.zeros((row_count, a_matrix.shape[0], a_matrix.shape[1]), jnp.float32)
    unused, (outputs, starts) = lax.scan(advance, start, pieces)
    return (merge_from_blocks(outputs), starts)


def scan_backward(
    starts, delta, b_rows, c_rows, scan_input_value, keep, d_state, a_matrix, row_count, length
):
    pieces = (starts,) + tuple(
        (
            to_blocks(value, row_count, length)
            for value in (delta, b_rows, c_rows, scan_input_value, keep, d_state)
        )
    )

    def retreat(adjoint_in, piece):
        start, delta_b, b_block, c_block, u_block, keep_b, d_block = piece
        decay, states = block_states(start, delta_b, b_block, u_block, keep_b, a_matrix)
        earlier = jnp.concatenate([start[:, None], states[:, :-1]], axis=1)
        source = c_block[:, :, :, None] * d_block[:, :, None, :]
        ahead = jnp.concatenate([decay[:, 1:], jnp.ones_like(decay[:, :1])], axis=1)
        unused, adjoint_steps = lax.scan(
            adjoint_step,
            adjoint_in,
            (jnp.moveaxis(ahead, 1, 0), jnp.moveaxis(source, 1, 0)),
            reverse=True,
            unroll=8,
        )
        adjoint = jnp.moveaxis(adjoint_steps, 0, 1)
        weighted = adjoint * earlier * decay
        pulled = jnp.sum(adjoint * b_block[:, :, :, None], axis=2)
        grad_amat = jnp.sum(weighted * delta_b[:, :, None, :], axis=(0, 1))
        grad_delta = jnp.sum(weighted * a_matrix, axis=2) + pulled * u_block
        grad_u = pulled * delta_b
        grad_b = jnp.sum(adjoint * (delta_b * u_block)[:, :, None, :], axis=3)
        grad_c = jnp.sum(states * d_block[:, :, None, :], axis=3)
        return (decay[:, 0] * adjoint[:, 0], (grad_amat, grad_delta, grad_u, grad_b, grad_c))

    start_adj = jnp.zeros((row_count, a_matrix.shape[0], a_matrix.shape[1]), jnp.float32)
    unused, outputs = lax.scan(retreat, start_adj, pieces, reverse=True)
    grad_amat = jnp.sum(outputs[0], axis=0)
    return (grad_amat,) + tuple((merge_from_blocks(value) for value in outputs[1:]))


def forward_pass(tokens, params, segment):
    in_low, x_low, dt_low, out_low, vec_low, gain_low = params
    row_count, length, width = tokens.shape
    inner_channel_width = x_low.shape[0]
    vector_f = vec_low.astype(jnp.float32)
    gain = gain_low.astype(jnp.float32)
    flat_in = tokens.reshape(row_count * length, width).astype(jnp.float32)
    inverse = lax.rsqrt(jnp.mean(flat_in * flat_in, axis=-1, keepdims=True) + NORM_EPS)
    normed = flat_in * inverse
    hidden = (normed * gain).astype(jnp.bfloat16)
    mixed = contract(hidden, in_low, 1, 1)
    x_part = mixed[:, :inner_channel_width].reshape(row_count, length, inner_channel_width)
    gate_in = mixed[:, inner_channel_width:]
    masks = lag_masks(segment)
    front = front_padded(x_part)
    conv_pre = vector_f[KCONV]
    for lag_index in range(KCONV):
        conv_pre = (
            conv_pre + vector_f[lag_index] * lag_view(front, lag_index, length) * masks[lag_index]
        )
    conv_flat = conv_pre.reshape(-1, inner_channel_width)
    u_low = jax.nn.silu(conv_flat).astype(jnp.bfloat16)
    scan_input_value = u_low.astype(jnp.float32)
    projected_values = jnp.dot(u_low, x_low, preferred_element_type=jnp.float32)
    dt_in = projected_values[:, :DTRANK].astype(jnp.bfloat16)
    b_rows = projected_values[:, DTRANK : DTRANK + DSTATE]
    c_rows = projected_values[:, DTRANK + DSTATE :]
    dt_pre = contract(dt_in, dt_low, 1, 1) + vector_f[KCONV + 1]
    delta = jax.nn.softplus(dt_pre)
    a_matrix = -jnp.exp(vector_f[KCONV + 3 :])
    keep = same_lag(segment, 1).reshape(-1)
    scanned, starts = scan_forward(
        delta, b_rows, c_rows, scan_input_value, keep, a_matrix, row_count, length
    )
    y_state = scanned + vector_f[KCONV + 2] * scan_input_value
    gate_act = jax.nn.silu(gate_in)
    gated = (y_state * gate_act).astype(jnp.bfloat16)
    result = flat_in + jnp.dot(gated, out_low, preferred_element_type=jnp.float32)
    saved = (
        normed,
        inverse,
        hidden,
        x_part,
        gate_in,
        conv_flat,
        u_low,
        dt_in,
        b_rows,
        c_rows,
        dt_pre,
        delta,
        keep,
        starts,
        y_state,
        gate_act,
        gated,
    )
    return (result.reshape(row_count, length, width), saved)


def backward_pass(tokens, out_grad, params, saved, segment):
    in_low, x_low, dt_low, out_low, vec_low, gain_low = params
    (
        normed,
        inverse,
        hidden,
        x_part,
        gate_in,
        conv_flat,
        u_low,
        dt_in,
        b_rows,
        c_rows,
        dt_pre,
        delta,
        keep,
        starts,
        y_state,
        gate_act,
        gated,
    ) = saved
    row_count, length, width = tokens.shape
    inner_channel_width = x_low.shape[0]
    vector_f = vec_low.astype(jnp.float32)
    gain = gain_low.astype(jnp.float32)
    a_matrix = -jnp.exp(vector_f[KCONV + 3 :])
    grad_flat = out_grad.reshape(row_count * length, width)
    d_gated = contract(grad_flat, out_low, 1, 1)
    grad_out = contract(gated, grad_flat, 0, 0)
    gate_sig = jax.nn.sigmoid(gate_in)
    d_state = d_gated * gate_act
    d_gate = d_gated * y_state * gate_sig * (1.0 + gate_in * (1.0 - gate_sig))
    scan_input_value = u_low.astype(jnp.float32)
    grad_skip = jnp.sum(d_state * scan_input_value, axis=0)
    grad_amat, d_delta, d_u_scan, d_b, d_c = scan_backward(
        starts, delta, b_rows, c_rows, scan_input_value, keep, d_state, a_matrix, row_count, length
    )
    d_u = d_state * vector_f[KCONV + 2] + d_u_scan
    d_dtpre = d_delta * jax.nn.sigmoid(dt_pre)
    grad_dtbias = jnp.sum(d_dtpre, axis=0)
    d_dtlow = d_dtpre.astype(jnp.bfloat16)
    d_dtin = jnp.dot(d_dtlow, dt_low, preferred_element_type=jnp.float32)
    grad_dt = contract(d_dtlow, dt_in, 0, 0)
    d_proj = jnp.concatenate([d_dtin, d_b, d_c], axis=1).astype(jnp.bfloat16)
    d_u = d_u + contract(d_proj, x_low, 1, 1)
    grad_x = contract(u_low, d_proj, 0, 0)
    conv_sig = jax.nn.sigmoid(conv_flat)
    d_conv = (d_u * conv_sig * (1.0 + conv_flat * (1.0 - conv_sig))).reshape(
        row_count, length, inner_channel_width
    )
    masks = lag_masks(segment)
    front = front_padded(x_part)
    rear = jnp.pad(d_conv, ((0, 0), (0, KCONV - 1), (0, 0)))
    d_xpart = jnp.zeros_like(d_conv)
    grad_taps = []
    for lag_index in range(KCONV):
        mask_ahead = jnp.pad(masks[lag_index], ((0, 0), (0, lag_index), (0, 0)))[:, lag_index:]
        d_xpart = d_xpart + vector_f[lag_index] * (
            rear[:, lag_index : lag_index + length] * mask_ahead
        )
        grad_taps.append(
            jnp.sum(d_conv * masks[lag_index] * lag_view(front, lag_index, length), axis=(0, 1))
        )
    grad_cbias = jnp.sum(d_conv, axis=(0, 1))
    d_mixed = jnp.concatenate([d_xpart.reshape(-1, inner_channel_width), d_gate], axis=1).astype(
        jnp.bfloat16
    )
    d_hidden = jnp.dot(d_mixed, in_low, preferred_element_type=jnp.float32)
    grad_in = contract(d_mixed, hidden, 0, 0)
    grad_gain = jnp.sum(d_hidden * normed, axis=0)
    d_normed = d_hidden * gain
    d_tokens = grad_flat.astype(jnp.float32) + inverse * (
        d_normed - normed * jnp.mean(d_normed * normed, axis=-1, keepdims=True)
    )
    grad_vec = jnp.concatenate(
        [
            jnp.stack(grad_taps),
            grad_cbias[None],
            grad_dtbias[None],
            grad_skip[None],
            grad_amat * a_matrix,
        ],
        axis=0,
    )
    return (
        d_tokens.reshape(row_count, length, width),
        (grad_in, grad_x, grad_dt, grad_out, grad_vec, grad_gain),
    )


def grams_by_groups(partials):
    shares = (
        lax.psum_scatter(partials[0], "ns", scatter_dimension=0, tiled=True),
        lax.psum_scatter(partials[1], "ns", scatter_dimension=0, tiled=True),
        lax.psum_scatter(partials[2], "ns", scatter_dimension=0, tiled=True),
        lax.psum_scatter(partials[3], "ns", scatter_dimension=0, tiled=True),
    )
    rounded_shares = tuple((share.astype(jnp.bfloat16) for share in shares))
    return (
        lax.all_gather(rounded_shares[0], "ns", axis=0, tiled=True),
        lax.all_gather(rounded_shares[1], "ns", axis=0, tiled=True),
        lax.all_gather(rounded_shares[2], "ns", axis=0, tiled=True),
        lax.all_gather(rounded_shares[3], "ns", axis=0, tiled=True),
    )


def newton_iterate(blocks, gram_maker):
    for step_index in range(NS_STEPS):
        partial_grams = tuple((contract(block, block, 0, 0) for block in blocks))
        grams = gram_maker(partial_grams)
        renewed = []
        for block, gram_low in zip(blocks, grams):
            square = jnp.dot(gram_low, gram_low, preferred_element_type=jnp.float32)
            poly = (COEF_B * gram_low.astype(jnp.float32) + COEF_C * square).astype(jnp.bfloat16)
            renewed.append(
                (
                    COEF_A * block.astype(jnp.float32)
                    + jnp.dot(block, poly, preferred_element_type=jnp.float32)
                ).astype(jnp.bfloat16)
            )
        blocks = tuple(renewed)
    return blocks


def adamw_update(param, first, second, grad):
    first_new = FIRST_MOMENT_BETA * first + (1.0 - FIRST_MOMENT_BETA) * grad
    second_new = BETA_SECOND * second + (1.0 - BETA_SECOND) * grad * grad
    first_hat = first_new / (1.0 - FIRST_MOMENT_BETA**STEP_NO)
    second_hat = second_new / (1.0 - BETA_SECOND**STEP_NO)
    param_new = param * (1.0 - ADAM_RATE * ADAM_DECAY) - ADAM_RATE * first_hat / (
        jnp.sqrt(second_hat) + ADAM_EPS
    )
    return (param_new, first_new, second_new)


def on_device(
    tokens,
    out_grad,
    doc_lengths,
    in_proj,
    inner_projection_weight,
    dt_proj,
    out_proj,
    in_moment,
    x_moment,
    dt_moment,
    out_moment,
    vectors,
    vector_first,
    vector_second,
    norm_gain,
    gain_first,
    gain_second,
):
    masters = (in_proj, inner_projection_weight, dt_proj, out_proj, vectors, norm_gain)
    lowered = tuple((master.astype(jnp.bfloat16) for master in masters))
    params = (
        lax.all_gather(lowered[0], ("fsdp", "ns"), axis=0, tiled=True),
        lax.all_gather(lowered[1], ("fsdp", "ns"), axis=0, tiled=True),
        lax.all_gather(lowered[2], ("fsdp", "ns"), axis=0, tiled=True),
        lax.all_gather(lowered[3], ("fsdp", "ns"), axis=0, tiled=True),
        lax.all_gather(lowered[4], ("fsdp", "ns"), axis=1, tiled=True),
        lax.all_gather(lowered[5], ("fsdp", "ns"), axis=0, tiled=True),
    )
    segment = segment_ids(doc_lengths, tokens.shape[1])
    block_out, saved = forward_pass(tokens, params, segment)
    back_params = (
        lax.all_gather(lowered[0], ("fsdp", "ns"), axis=0, tiled=True),
        lax.all_gather(lowered[1], ("fsdp", "ns"), axis=0, tiled=True),
        lax.all_gather(lowered[2], ("fsdp", "ns"), axis=0, tiled=True),
        lax.all_gather(lowered[3], ("fsdp", "ns"), axis=0, tiled=True),
        lax.all_gather(lowered[4], ("fsdp", "ns"), axis=1, tiled=True),
        lax.all_gather(lowered[5], ("fsdp", "ns"), axis=0, tiled=True),
    )
    unused, back_saved = forward_pass(tokens, back_params, segment)
    grad_tokens, grads = backward_pass(tokens, out_grad, back_params, back_saved, segment)
    summed = (
        lax.psum_scatter(grads[0], ("fsdp", "ns"), scatter_dimension=0, tiled=True),
        lax.psum_scatter(grads[1], ("fsdp", "ns"), scatter_dimension=0, tiled=True),
        lax.psum_scatter(grads[2], ("fsdp", "ns"), scatter_dimension=0, tiled=True),
        lax.psum_scatter(grads[3], ("fsdp", "ns"), scatter_dimension=0, tiled=True),
        lax.psum_scatter(grads[4], ("fsdp", "ns"), scatter_dimension=1, tiled=True),
        lax.psum_scatter(grads[5], ("fsdp", "ns"), scatter_dimension=0, tiled=True),
    )
    old_moments = (in_moment, x_moment, dt_moment, out_moment)
    moments = tuple((MOMENTUM * moment + grad for moment, grad in zip(old_moments, summed[:4])))
    squares = lax.psum(tuple((jnp.sum(moment * moment) for moment in moments)), ("fsdp", "ns"))
    scaled = tuple(
        (
            (moment / (jnp.sqrt(total) + FROB_EPS)).astype(jnp.bfloat16)
            for moment, total in zip(moments, squares)
        )
    )
    weights = (in_proj, inner_projection_weight, dt_proj, out_proj)
    blocks = jax.tree.map(
        lambda part, own: part.astype(own.dtype),
        lax.all_gather(as_sent(scaled), "fsdp", axis=0, tiled=True),
        scaled,
    )
    finals = newton_iterate(blocks, grams_by_groups)
    position = lax.axis_index("fsdp")
    own_blocks = tuple(
        (
            lax.dynamic_slice_in_dim(block, position * weight.shape[0], weight.shape[0], 0)
            for block, weight in zip(finals, weights)
        )
    )
    devices = lax.axis_size("fsdp") * lax.axis_size("ns")
    fans = (DMODEL, DINNER, DTRANK, DINNER // 8)
    results = []
    for weight, moment, block, fan in zip(weights, moments, own_blocks, fans):
        per_dev = weight.shape[0]
        rate = 0.5 * math.sqrt(per_dev * devices / fan)
        results.append((1.0 - SHRINK) * weight - rate * block.astype(jnp.float32))
        results.append(moment)
    vec_new, vec_first, vec_second = adamw_update(vectors, vector_first, vector_second, summed[4])
    gain_new, gain_m, gain_v = adamw_update(norm_gain, gain_first, gain_second, summed[5])
    return (
        block_out,
        grad_tokens,
        results[0],
        results[1],
        results[2],
        results[3],
        results[4],
        results[5],
        results[6],
        results[7],
        vec_new,
        vec_first,
        vec_second,
        gain_new,
        gain_m,
        gain_v,
    )


def solution(mesh):
    placed = (
        P(("fsdp", "ns"), None, None),
        P(("fsdp", "ns"), None, None),
        P(("fsdp", "ns"), None),
        P(("fsdp", "ns"), None),
        P(("fsdp", "ns"), None),
        P(("fsdp", "ns"), None),
        P(("fsdp", "ns"), None),
        P(("fsdp", "ns"), None),
        P(("fsdp", "ns"), None),
        P(("fsdp", "ns"), None),
        P(("fsdp", "ns"), None),
        P(None, ("fsdp", "ns")),
        P(None, ("fsdp", "ns")),
        P(None, ("fsdp", "ns")),
        P(("fsdp", "ns")),
        P(("fsdp", "ns")),
        P(("fsdp", "ns")),
    )
    return jax.shard_map(
        on_device,
        mesh=mesh,
        in_specs=placed,
        out_specs=(
            P(("fsdp", "ns"), None, None),
            P(("fsdp", "ns"), None, None),
            P(("fsdp", "ns"), None),
            P(("fsdp", "ns"), None),
            P(("fsdp", "ns"), None),
            P(("fsdp", "ns"), None),
            P(("fsdp", "ns"), None),
            P(("fsdp", "ns"), None),
            P(("fsdp", "ns"), None),
            P(("fsdp", "ns"), None),
            P(None, ("fsdp", "ns")),
            P(None, ("fsdp", "ns")),
            P(None, ("fsdp", "ns")),
            P(("fsdp", "ns")),
            P(("fsdp", "ns")),
            P(("fsdp", "ns")),
        ),
        check_vma=False,
    )
```

profile of v0, /device:TPU:0, one launch (start us, length us, event | category | flops | bytes accessed | tf_op | source)
XLA Modules:
  0.0 3830.9 jit_solution(8966683945728612808)
XLA Ops:
  11.7 42.7 %all-reduce.9 = bf16[1024]{0:T(1024)(128)(2,1)S(1)} all-reduce(bf16[1024]{0:T(1024)(128)(2,1)S(1)} %dynamic-update-slice), channel_id=1, replica_groups=mesh['fsdp'=8,'ns'=4] {'fsdp','ns'}, use_global_device_ids=true, to_apply=%add.9 | all-reduce | flops 1024 | bytes 4096
  55.1 68.9 %all-gather = bf16[32,64,23]{1,2,0:T(8,128)(2,1)S(1)} all-gather(bf16[1,64,23]{1,2,0:T(8,128)(2,1)S(1)} %convert_bitcast_fusion), channel_id=1, replica_groups=mesh['fsdp'=8,'ns'=4] {'fsdp','ns'}, dimensions={0}, use_global_device_ids=true | all-gather | bytes 97152 | tf_op jit(solution)/shard_map/all_gather | solution.py:383
  126.4 73.0 %all_gather.88 = bf16[2048,64]{1,0:T(8,128)(2,1)} all-gather(bf16[64,64]{1,0:T(8,128)(2,1)S(1)} %convert_element_type.407), channel_id=1, replica_groups=mesh['fsdp'=8,'ns'=4] {'fsdp','ns'}, dimensions={0}, use_global_device_ids=true | all-gather | bytes 270336 | tf_op jit(solution)/shard_map/all_gather | solution.py:381
  199.6 69.8 %all_gather.87 = bf16[2048,96]{1,0:T(8,128)(2,1)S(1)} all-gather(bf16[64,96]{1,0:T(8,128)(2,1)S(1)} %convert_element_type.406), channel_id=1, replica_groups=mesh['fsdp'=8,'ns'=4] {'fsdp','ns'}, dimensions={0}, use_global_device_ids=true | all-gather | bytes 405504 | tf_op jit(solution)/shard_map/all_gather | solution.py:380
  299.6 376.3 %while.140 = (s32[]{:T(128)}, f32[1,16,2048]{2,1,0:T(8,128)S(1)}, f32[4,1,64,2048]{3,2,1,0:T(8,128)}, f32[4,1,16,2048]{3,2,1,0:T(8,128)}, f32[4,1,64,2048]{3,2,1...) while((s32[]{:T(128)}, f32[1,16,2048]{2,1,0:T(8,128)S(1)}, ...), condition=%wide.region_12.13_spmd, body=%wide.region_8.12_spmd.sunk | while | flops 11075594 | bytes 40922568 | solution.py:119
  311.8 73.9 %while.145 = (s32[]{:T(128)}, f32[1,16,2048]{2,1,0:T(8,128)S(1)}, f32[8,8,1,16,2048]{4,3,1,2,0:T(8,128)}, f32[8,8,1,16,2048]{4,3,2,1,0:T(8,128)}, f32[8,8,1,16,2...) while((s32[]{:T(128)}, f32[1,16,2048]{2,1,0:T(8,128)S(1)}, ...), condition=%wide.region_10.10_spmd, body=%wide.region_9.9_spmd.sunk | while | flops 589832 | bytes 7471893 | solution.py:99
  405.9 73.9 %while.145 = (s32[]{:T(128)}, f32[1,16,2048]{2,1,0:T(8,128)S(1)}, f32[8,8,1,16,2048]{4,3,1,2,0:T(8,128)}, f32[8,8,1,16,2048]{4,3,2,1,0:T(8,128)}, f32[8,8,1,16,2...) while((s32[]{:T(128)}, f32[1,16,2048]{2,1,0:T(8,128)S(1)}, ...), condition=%wide.region_10.10_spmd, body=%wide.region_9.9_spmd.sunk | while | flops 589832 | bytes 7471893 | solution.py:99
  500.0 73.9 %while.145 = (s32[]{:T(128)}, f32[1,16,2048]{2,1,0:T(8,128)S(1)}, f32[8,8,1,16,2048]{4,3,1,2,0:T(8,128)}, f32[8,8,1,16,2048]{4,3,2,1,0:T(8,128)}, f32[8,8,1,16,2...) while((s32[]{:T(128)}, f32[1,16,2048]{2,1,0:T(8,128)S(1)}, ...), condition=%wide.region_10.10_spmd, body=%wide.region_9.9_spmd.sunk | while | flops 589832 | bytes 7471893 | solution.py:99
  594.0 73.9 %while.145 = (s32[]{:T(128)}, f32[1,16,2048]{2,1,0:T(8,128)S(1)}, f32[8,8,1,16,2048]{4,3,1,2,0:T(8,128)}, f32[8,8,1,16,2048]{4,3,2,1,0:T(8,128)}, f32[8,8,1,16,2...) while((s32[]{:T(128)}, f32[1,16,2048]{2,1,0:T(8,128)S(1)}, ...), condition=%wide.region_10.10_spmd, body=%wide.region_9.9_spmd.sunk | while | flops 589832 | bytes 7471893 | solution.py:99
  681.9 660.0 %while.143 = (s32[]{:T(128)}, f32[1,16,2048]{2,1,0:T(8,128)}, f32[4,16,2048]{2,1,0:T(8,128)}, f32[4,1,64,2048]{3,2,1,0:T(8,128)}, f32[4,1,64,2048]{3,2,1,0:T(8,1...) while((s32[]{:T(128)}, f32[1,16,2048]{2,1,0:T(8,128)}, ...), condition=%wide.region_23.24_spmd, body=%wide.region_13.23_spmd.sunk | while | flops 45414420 | bytes 240885808 | solution.py:157
  703.5 73.9 %while.146 = (s32[]{:T(128)}, f32[1,16,2048]{2,1,0:T(8,128)S(1)}, f32[8,8,1,16,2048]{4,3,1,2,0:T(8,128)}, f32[8,8,1,16,2048]{4,3,2,1,0:T(8,128)}, f32[8,8,1,16,2...) while((s32[]{:T(128)}, f32[1,16,2048]{2,1,0:T(8,128)S(1)}, ...), condition=%wide.region_17.17_spmd, body=%wide.region_16.16_spmd.sunk | while | flops 589832 | bytes 7471893 | solution.py:99
  797.6 23.7 while.147
  868.3 73.9 %while.146 = (s32[]{:T(128)}, f32[1,16,2048]{2,1,0:T(8,128)S(1)}, f32[8,8,1,16,2048]{4,3,1,2,0:T(8,128)}, f32[8,8,1,16,2048]{4,3,2,1,0:T(8,128)}, f32[8,8,1,16,2...) while((s32[]{:T(128)}, f32[1,16,2048]{2,1,0:T(8,128)S(1)}, ...), condition=%wide.region_17.17_spmd, body=%wide.region_16.16_spmd.sunk | while | flops 589832 | bytes 7471893 | solution.py:99
  962.4 23.7 while.147
  1033.1 73.9 %while.146 = (s32[]{:T(128)}, f32[1,16,2048]{2,1,0:T(8,128)S(1)}, f32[8,8,1,16,2048]{4,3,1,2,0:T(8,128)}, f32[8,8,1,16,2048]{4,3,2,1,0:T(8,128)}, f32[8,8,1,16,2...) while((s32[]{:T(128)}, f32[1,16,2048]{2,1,0:T(8,128)S(1)}, ...), condition=%wide.region_17.17_spmd, body=%wide.region_16.16_spmd.sunk | while | flops 589832 | bytes 7471893 | solution.py:99
  1127.2 23.7 while.147
  1198.0 73.9 %while.146 = (s32[]{:T(128)}, f32[1,16,2048]{2,1,0:T(8,128)S(1)}, f32[8,8,1,16,2048]{4,3,1,2,0:T(8,128)}, f32[8,8,1,16,2048]{4,3,2,1,0:T(8,128)}, f32[8,8,1,16,2...) while((s32[]{:T(128)}, f32[1,16,2048]{2,1,0:T(8,128)S(1)}, ...), condition=%wide.region_17.17_spmd, body=%wide.region_16.16_spmd.sunk | while | flops 589832 | bytes 7471893 | solution.py:99
  1292.1 23.7 while.147
  1351.6 373.3 %while.138 = (s32[]{:T(128)}, f32[1,16,2048]{2,1,0:T(8,128)S(1)}, f32[4,1,64,2048]{3,2,1,0:T(8,128)}, f32[4,1,64,2048]{3,2,1,0:T(8,128)S(1)}, f32[16,2048]{1,0:T...) while((s32[]{:T(128)}, f32[1,16,2048]{2,1,0:T(8,128)S(1)}, ...), condition=%wide.region_7.8_spmd, body=%wide.region_3.7_spmd.sunk | while | flops 11075594 | bytes 39349128 | solution.py:119
  1363.6 74.0 %while.144 = (s32[]{:T(128)}, f32[1,16,2048]{2,1,0:T(8,128)S(1)}, f32[8,8,1,16,2048]{4,3,1,2,0:T(8,128)}, f32[8,8,1,16,2048]{4,3,2,1,0:T(8,128)}, f32[8,8,1,16,2...) while((s32[]{:T(128)}, f32[1,16,2048]{2,1,0:T(8,128)S(1)}, ...), condition=%wide.region_5.5_spmd, body=%wide.region_4.4_spmd.sunk | while | flops 589832 | bytes 7471893 | solution.py:99
  1457.1 73.9 %while.144 = (s32[]{:T(128)}, f32[1,16,2048]{2,1,0:T(8,128)S(1)}, f32[8,8,1,16,2048]{4,3,1,2,0:T(8,128)}, f32[8,8,1,16,2048]{4,3,2,1,0:T(8,128)}, f32[8,8,1,16,2...) while((s32[]{:T(128)}, f32[1,16,2048]{2,1,0:T(8,128)S(1)}, ...), condition=%wide.region_5.5_spmd, body=%wide.region_4.4_spmd.sunk | while | flops 589832 | bytes 7471893 | solution.py:99
  1550.4 73.9 %while.144 = (s32[]{:T(128)}, f32[1,16,2048]{2,1,0:T(8,128)S(1)}, f32[8,8,1,16,2048]{4,3,1,2,0:T(8,128)}, f32[8,8,1,16,2048]{4,3,2,1,0:T(8,128)}, f32[8,8,1,16,2...) while((s32[]{:T(128)}, f32[1,16,2048]{2,1,0:T(8,128)S(1)}, ...), condition=%wide.region_5.5_spmd, body=%wide.region_4.4_spmd.sunk | while | flops 589832 | bytes 7471893 | solution.py:99
  1643.6 73.9 %while.144 = (s32[]{:T(128)}, f32[1,16,2048]{2,1,0:T(8,128)S(1)}, f32[8,8,1,16,2048]{4,3,1,2,0:T(8,128)}, f32[8,8,1,16,2048]{4,3,2,1,0:T(8,128)}, f32[8,8,1,16,2...) while((s32[]{:T(128)}, f32[1,16,2048]{2,1,0:T(8,128)S(1)}, ...), condition=%wide.region_5.5_spmd, body=%wide.region_4.4_spmd.sunk | while | flops 589832 | bytes 7471893 | solution.py:99
  1769.1 94.4 %reduce-scatter.42.cloned.1.call-done = f32[64,96]{1,0:T(8,128)} async-done(((f32[2048,96]{1,0:T(8,128)}), f32[64,96]{1,0:T(8,128)}) %reduce-scatter.42.cloned.1.call-update) | async-done | bytes 24592 | tf_op jit(solution)/shard_map/reduce_scatter | solution.py:400
  1864.8 183.2 %reduce-scatter.54.cloned.1.call-done = f32[64,1024]{1,0:T(8,128)} async-done(((f32[2048,1024]{1,0:T(8,128)}), f32[64,1024]{1,0:T(8,128)}) %reduce-scatter.54.cloned.1.call-update) | async-done | bytes 262160 | tf_op jit(solution)/shard_map/reduce_scatter | solution.py:402
  2049.6 362.4 %reduce-scatter.32.cloned.1.call-done = f32[128,1024]{1,0:T(8,128)} async-done(((f32[4096,1024]{1,0:T(8,128)}), f32[128,1024]{1,0:T(8,128)}) %reduce-scatter.32.cloned.1.call-update) | async-done | bytes 524304 | tf_op jit(solution)/shard_map/reduce_scatter | solution.py:399
  2414.0 38.6 %all-reduce.15 = (f32[]{:T(128)}, f32[]{:T(128)}, f32[]{:T(128)}, f32[]{:T(128)}, f32[1024]{0:T(1024)S(1)}) all-reduce(f32[]{:T(128)} %get-tuple-element.1071, f32[]{:T(128)} %get-tuple-element.1069, f32[]{:T(128)} %get-tuple-element.1067, f32[]{:T(128)} %get-tuple-element.1065, ...), channel_id=1, replica_groups=mesh['fsdp'=8,'ns'=4] {'fsdp','ns'}, use_global_device_ids=true, to_apply=%region_27.28 | all-reduce | flops 1028 | bytes 8224 | tf_op jit(solution)/shard_map/psum | solution.py:408
  2455.6 22.0 all-gather.28.cloned.1.call-done
  2482.5 25.4 all-gather.18.cloned.1.call-done
  2514.8 72.2 %reduce-scatter.56.cloned.1.call-done = f32[256,1024]{1,0:T(8,128)} async-done(((f32[1024,1024]{1,0:T(8,128)}), f32[256,1024]{1,0:T(8,128)}) %reduce-scatter.56.cloned.1.call-update) | async-done | bytes 1048592 | tf_op jit(solution)/shard_map/reduce_scatter | solution.py:317
  2589.3 77.3 %reduce-scatter.34.cloned.1.call-done = f32[256,1024]{1,0:T(8,128)} async-done(((f32[1024,1024]{1,0:T(8,128)}), f32[256,1024]{1,0:T(8,128)}) %reduce-scatter.34.cloned.1.call-update) | async-done | bytes 1048592 | tf_op jit(solution)/shard_map/reduce_scatter | solution.py:314
  2669.2 45.5 %all-gather.30.cloned.1.call-done = bf16[1024,1024]{1,0:T(8,128)(2,1)} async-done(((bf16[256,1024]{1,0:T(8,128)(2,1)}), bf16[1024,1024]{1,0:T(8,128)(2,1)}) %all-gather.30.cloned.1.call-update) | async-done | bytes 2097168 | tf_op jit(solution)/shard_map/all_gather | solution.py:324
  2724.5 36.8 all-gather.20.cloned.1.call-done
  2778.4 60.7 %reduce-scatter.58.cloned.1.call-done = f32[256,1024]{1,0:T(8,128)} async-done(((f32[1024,1024]{1,0:T(8,128)}), f32[256,1024]{1,0:T(8,128)}) %reduce-scatter.58.cloned.1.call-update) | async-done | bytes 1048592 | tf_op jit(solution)/shard_map/reduce_scatter | solution.py:317
  2841.3 77.4 %reduce-scatter.36.cloned.1.call-done = f32[256,1024]{1,0:T(8,128)} async-done(((f32[1024,1024]{1,0:T(8,128)}), f32[256,1024]{1,0:T(8,128)}) %reduce-scatter.36.cloned.1.call-update) | async-done | bytes 1048592 | tf_op jit(solution)/shard_map/reduce_scatter | solution.py:314
  2942.6 24.0 all-gather.32.cloned.1.call-done
  2976.5 36.8 all-gather.22.cloned.1.call-done
  3068.6 62.3 %reduce-scatter.60.cloned.1.call-done = f32[256,1024]{1,0:T(8,128)} async-done(((f32[1024,1024]{1,0:T(8,128)}), f32[256,1024]{1,0:T(8,128)}) %reduce-scatter.60.cloned.1.call-update) | async-done | bytes 1048592 | tf_op jit(solution)/shard_map/reduce_scatter | solution.py:317
  3133.1 77.3 %reduce-scatter.38.cloned.1.call-done = f32[256,1024]{1,0:T(8,128)} async-done(((f32[1024,1024]{1,0:T(8,128)}), f32[256,1024]{1,0:T(8,128)}) %reduce-scatter.38.cloned.1.call-update) | async-done | bytes 1048592 | tf_op jit(solution)/shard_map/reduce_scatter | solution.py:314
  3212.5 20.1 reduce-scatter.48.cloned.1.call-done
  3268.0 30.5 all-gather.34.cloned.1.call-done
  3308.3 36.9 all-gather.24.cloned.1.call-done
  3400.7 62.1 %reduce-scatter.62.cloned.1.call-done = f32[256,1024]{1,0:T(8,128)} async-done(((f32[1024,1024]{1,0:T(8,128)}), f32[256,1024]{1,0:T(8,128)}) %reduce-scatter.62.cloned.1.call-update) | async-done | bytes 1048592 | tf_op jit(solution)/shard_map/reduce_scatter | solution.py:317
  3465.3 77.2 %reduce-scatter.40.cloned.1.call-done = f32[256,1024]{1,0:T(8,128)} async-done(((f32[1024,1024]{1,0:T(8,128)}), f32[256,1024]{1,0:T(8,128)}) %reduce-scatter.40.cloned.1.call-update) | async-done | bytes 1048592 | tf_op jit(solution)/shard_map/reduce_scatter | solution.py:314
  3551.9 128.6 %reduce-scatter.64.cloned.1.call-done = f32[64,23]{1,0:T(8,128)} async-done(((f32[2048,23]{1,0:T(8,128)}), f32[64,23]{1,0:T(8,128)}) %reduce-scatter.64.cloned.1.call-update) | async-done | bytes 5904
  3682.6 16.2 reduce-scatter.52.cloned.1.call-done
  3733.6 31.0 all-gather.36.cloned.1.call-done
  3771.9 39.5 %all-gather.26.cloned.1.call-done = bf16[1024,1024]{1,0:T(8,128)(2,1)} async-done(((bf16[256,1024]{1,0:T(8,128)(2,1)}), bf16[1024,1024]{1,0:T(8,128)(2,1)}) %all-gather.26.cloned.1.call-update) | async-done | bytes 2097168 | tf_op jit(solution)/shard_map/all_gather | solution.py:321
  (1833 shorter events, 1814.2 us)
Async XLA Ops:
  7.2 192.2 %copy-start.20 = (bf16[1,256,1024]{2,1,0:T(8,128)(2,1)S(1)}, bf16[1,256,1024]{2,1,0:T(8,128)(2,1)}, u32[]{:S(2)}) copy-start(bf16[1,256,1024]{2,1,0:T(8,128)(2,1)} %param.31) | copy-start | bytes 1572868
  7.2 263.0 %all-gather.14.cloned.1.call-start = ((), (), s32[]{:S(2)}) async-start(), calls=%async_computation.21 | async-start | bytes 8650752 | tf_op jit(solution)/shard_map/all_gather | solution.py:379
  9.1 269.2 %all-gather.16.cloned.1.call-start = ((), (), s32[]{:S(2)}) async-start(), calls=%async_computation.22 | async-start | bytes 4325376 | tf_op jit(solution)/shard_map/all_gather | solution.py:382
  10.8 1756.9 %reduce-scatter.44.cloned.1.call-start = ((), (), s32[]{:S(2)}) async-start(), calls=%async_computation.34 | async-start | bytes 1081344 | tf_op jit(solution)/shard_map/reduce_scatter | solution.py:401
  54.4 215.9 %copy-start.51 = (f32[1024]{0:T(1024)}, f32[1024]{0:T(1024)S(1)}, u32[]{:S(2)}) copy-start(f32[1024]{0:T(1024)S(1)} %convert_element_type.398) | copy-start | bytes 12292
  124.2 146.1 %copy-start.34 = (f32[2048,23]{0,1:T(8,128)}, f32[2048,23]{0,1:T(8,128)S(1)}, u32[]{:S(2)}) copy-start(f32[2048,23]{0,1:T(8,128)S(1)} %reshape.767) | copy-start | bytes 565252
  125.8 152.6 %copy-start.69 = (f32[1,256]{1,0:T(1,128)}, f32[1,256]{1,0:T(1,128)S(1)}, u32[]{:S(2)}) copy-start(f32[1,256]{1,0:T(1,128)S(1)} %get-tuple-element.1074) | copy-start | bytes 3076
  681.9 660.0 %copy-start.63 = (f32[1,2048]{1,0:T(1,128)S(1)}, f32[1,2048]{1,0:T(1,128)}, u32[]{:S(2)}) copy-start(f32[1,2048]{1,0:T(1,128)} %get-tuple-element.1097) | copy-start | bytes 24580
  1349.9 513.5 %reduce-scatter.42.cloned.1.call-start = ((), (), s32[]{:S(2)}) async-start(), calls=%async_computation.33 | async-start | bytes 1081344 | tf_op jit(solution)/shard_map/reduce_scatter | solution.py:400
  1730.1 317.9 %reduce-scatter.54.cloned.1.call-start = ((), (), s32[]{:S(2)}) async-start(), calls=%async_computation.39 | async-start | bytes 8650752 | tf_op jit(solution)/shard_map/reduce_scatter | solution.py:402
  1742.8 669.3 %reduce-scatter.32.cloned.1.call-start = ((), (), s32[]{:S(2)}) async-start(), calls=%async_computation.23 | async-start | bytes 17301504 | tf_op jit(solution)/shard_map/reduce_scatter | solution.py:399
  1759.5 288.5 %copy-start.43 = (f32[64,1024]{1,0:T(8,128)S(1)}, f32[64,1024]{1,0:T(8,128)}, u32[]{:S(2)}) copy-start(f32[64,1024]{1,0:T(8,128)} %param.41) | copy-start | bytes 786436
  1759.5 718.1 %all-gather.28.cloned.1.call-start = ((), (), s32[]{:S(2)}) async-start(), calls=%async_computation.40 | async-start | bytes 1179648 | tf_op jit(solution)/shard_map/all_gather | solution.py:418
  1769.1 1153.2 %copy-start.48 = (f32[64,64]{1,0:T(8,128)}, f32[64,64]{1,0:T(8,128)S(1)}, u32[]{:S(2)}) copy-start(f32[64,64]{1,0:T(8,128)S(1)} %get-tuple-element.1068) | copy-start | bytes 49156
  1864.8 1066.6 %copy-start.49 = (f32[64,96]{1,0:T(8,128)}, f32[64,96]{1,0:T(8,128)S(1)}, u32[]{:S(2)}) copy-start(f32[64,96]{1,0:T(8,128)S(1)} %get-tuple-element.1070) | copy-start | bytes 73732
  2049.6 432.8 %copy-start.40 = (f32[64,1024]{1,0:T(8,128)}, f32[64,1024]{1,0:T(8,128)S(1)}, u32[]{:S(2)}) copy-start(f32[64,1024]{1,0:T(8,128)S(1)} %get-tuple-element.1066) | copy-start | bytes 786436
  2454.0 54.0 %all-gather.18.cloned.1.call-start = ((), (), s32[]{:S(2)}) async-start(), calls=%async_computation.24 | async-start | bytes 2359296 | tf_op jit(solution)/shard_map/all_gather | solution.py:418
  2455.5 131.6 %reduce-scatter.56.cloned.1.call-start = ((), (), s32[]{:S(2)}) async-start(), calls=%async_computation.41 | async-start | bytes 5242880 | tf_op jit(solution)/shard_map/reduce_scatter | solution.py:317
  2482.5 184.1 %reduce-scatter.34.cloned.1.call-start = ((), (), s32[]{:S(2)}) async-start(), calls=%async_computation.25 | async-start | bytes 5242880 | tf_op jit(solution)/shard_map/reduce_scatter | solution.py:314
  2514.8 199.9 %copy-start.19 = (bf16[512,1024]{1,0:T(8,128)(2,1)S(1)}, bf16[512,1024]{1,0:T(8,128)(2,1)}, u32[]{:S(2)}) copy-start(bf16[512,1024]{1,0:T(8,128)(2,1)} %all-gather.28.cloned.1.call-done) | copy-start | bytes 3145732
  2514.8 199.9 %all-gather.30.cloned.1.call-start = ((), (), s32[]{:S(2)}) async-start(), calls=%async_computation.42 | async-start | bytes 2621440 | tf_op jit(solution)/shard_map/all_gather | solution.py:324
  2589.2 172.1 %all-gather.20.cloned.1.call-start = ((), (), s32[]{:S(2)}) async-start(), calls=%async_computation.26 | async-start | bytes 2621440 | tf_op jit(solution)/shard_map/all_gather | solution.py:321
  2668.7 170.4 %reduce-scatter.58.cloned.1.call-start = ((), (), s32[]{:S(2)}) async-start(), calls=%async_computation.43 | async-start | bytes 5242880 | tf_op jit(solution)/shard_map/reduce_scatter | solution.py:317
  2724.5 194.2 %reduce-scatter.36.cloned.1.call-start = ((), (), s32[]{:S(2)}) async-start(), calls=%async_computation.27 | async-start | bytes 5242880 | tf_op jit(solution)/shard_map/reduce_scatter | solution.py:314
  2778.3 188.2 %all-gather.32.cloned.1.call-start = ((), (), s32[]{:S(2)}) async-start(), calls=%async_computation.44 | async-start | bytes 2621440 | tf_op jit(solution)/shard_map/all_gather | solution.py:324
  2841.3 172.0 %all-gather.22.cloned.1.call-start = ((), (), s32[]{:S(2)}) async-start(), calls=%async_computation.28 | async-start | bytes 2621440 | tf_op jit(solution)/shard_map/all_gather | solution.py:321
  2920.8 112.7 %reduce-scatter.46.cloned.1.call-start = ((), (), s32[]{:S(2)}) async-start(), calls=%async_computation.35 | async-start | bytes 40960 | tf_op jit(solution)/shard_map/reduce_scatter | solution.py:316
  2941.5 112.0 %reduce-scatter.66.cloned.1.call-start = ((), (), s32[]{:S(2)}) async-start(), calls=%async_computation.50 | async-start | bytes 61440
  2942.4 188.5 %reduce-scatter.60.cloned.1.call-start = ((), (), s32[]{:S(2)}) async-start(), calls=%async_computation.45 | async-start | bytes 5242880 | tf_op jit(solution)/shard_map/reduce_scatter | solution.py:317
  2976.4 233.9 %reduce-scatter.38.cloned.1.call-start = ((), (), s32[]{:S(2)}) async-start(), calls=%async_computation.29 | async-start | bytes 5242880 | tf_op jit(solution)/shard_map/reduce_scatter | solution.py:314
  3030.6 202.0 %reduce-scatter.48.cloned.1.call-start = ((), (), s32[]{:S(2)}) async-start(), calls=%async_computation.36 | async-start | bytes 40960 | tf_op jit(solution)/shard_map/reduce_scatter | solution.py:316
  3048.5 204.2 %reduce-scatter.68.cloned.1.call-start = ((), (), s32[]{:S(2)}) async-start(), calls=%async_computation.51 | async-start | bytes 61440
  3068.6 229.9 %all-gather.34.cloned.1.call-start = ((), (), s32[]{:S(2)}) async-start(), calls=%async_computation.46 | async-start | bytes 2621440 | tf_op jit(solution)/shard_map/all_gather | solution.py:324
  3133.0 212.2 %all-gather.24.cloned.1.call-start = ((), (), s32[]{:S(2)}) async-start(), calls=%async_computation.30 | async-start | bytes 2621440 | tf_op jit(solution)/shard_map/all_gather | solution.py:321
  3212.4 153.2 %reduce-scatter.50.cloned.1.call-start = ((), (), s32[]{:S(2)}) async-start(), calls=%async_computation.37 | async-start | bytes 40960 | tf_op jit(solution)/shard_map/reduce_scatter | solution.py:316
  3247.5 138.0 %reduce-scatter.70.cloned.1.call-start = ((), (), s32[]{:S(2)}) async-start(), calls=%async_computation.52 | async-start | bytes 61440
  3267.7 195.1 %reduce-scatter.62.cloned.1.call-start = ((), (), s32[]{:S(2)}) async-start(), calls=%async_computation.47 | async-start | bytes 5242880 | tf_op jit(solution)/shard_map/reduce_scatter | solution.py:317
  3308.2 234.2 %reduce-scatter.40.cloned.1.call-start = ((), (), s32[]{:S(2)}) async-start(), calls=%async_computation.31 | async-start | bytes 5242880 | tf_op jit(solution)/shard_map/reduce_scatter | solution.py:314
  3362.2 318.3 %reduce-scatter.64.cloned.1.call-start = ((), (), s32[]{:S(2)}) async-start(), calls=%async_computation.49 | async-start | bytes 1081344
  3365.0 333.9 %reduce-scatter.52.cloned.1.call-start = ((), (), s32[]{:S(2)}) async-start(), calls=%async_computation.38 | async-start | bytes 40960 | tf_op jit(solution)/shard_map/reduce_scatter | solution.py:316
  3380.6 338.2 %reduce-scatter.72.cloned.1.call-start = ((), (), s32[]{:S(2)}) async-start(), calls=%async_computation.53 | async-start | bytes 61440
  3400.6 143.9 %copy-start.30 = (bf16[1,256,1024]{2,1,0:T(8,128)(2,1)S(1)}, bf16[1,256,1024]{2,1,0:T(8,128)(2,1)}, u32[]{:S(2)}) copy-start(bf16[1,256,1024]{2,1,0:T(8,128)(2,1)} %param.32) | copy-start | bytes 1572868
  3400.6 364.0 %all-gather.36.cloned.1.call-start = ((), (), s32[]{:S(2)}) async-start(), calls=%async_computation.48 | async-start | bytes 2621440 | tf_op jit(solution)/shard_map/all_gather | solution.py:324
  3464.9 346.5 %all-gather.26.cloned.1.call-start = ((), (), s32[]{:S(2)}) async-start(), calls=%async_computation.32 | async-start | bytes 2621440 | tf_op jit(solution)/shard_map/all_gather | solution.py:321
  3547.1 134.9 %copy-start.76 = (f32[32]{0:T(128)S(1)}, f32[32]{0:T(128)}, u32[]{:S(2)}) copy-start(f32[32]{0:T(128)} %param.45) | copy-start | bytes 388
  3547.1 134.9 %copy-start.77 = (f32[32]{0:T(128)S(1)}, f32[32]{0:T(128)}, u32[]{:S(2)}) copy-start(f32[32]{0:T(128)} %param.46) | copy-start | bytes 388
  3547.1 165.9 %copy-start.45 = (f32[64,64]{1,0:T(8,128)S(1)}, f32[64,64]{1,0:T(8,128)}, u32[]{:S(2)}) copy-start(f32[64,64]{1,0:T(8,128)} %param.36) | copy-start | bytes 49156
  3547.1 185.9 %copy-start.47 = (f32[64,96]{1,0:T(8,128)S(1)}, f32[64,96]{1,0:T(8,128)}, u32[]{:S(2)}) copy-start(f32[64,96]{1,0:T(8,128)} %param.35) | copy-start | bytes 73732
  (124 other events, 1822.3 us)
Sparse Core Ops, SparseCore 0:
  11.6 80.8 all-gather.13
  96.1 61.9 all-gather.15
  1350.0 133.0 reduce-scatter.43
  1730.2 133.1 reduce-scatter.41
  1865.6 182.3 reduce-scatter.53
  2050.2 361.8 reduce-scatter.31
  2454.1 23.4 all-gather.27
  2480.0 27.8 all-gather.17
  2510.3 76.7 reduce-scatter.55
  2589.3 77.2 reduce-scatter.33
  2668.2 46.4 all-gather.29
  2716.6 44.6 all-gather.19
  2763.6 75.4 reduce-scatter.57
  2841.4 77.2 reduce-scatter.35
  2920.1 46.4 all-gather.31
  2968.6 44.6 all-gather.21
  3015.9 17.5 reduce-scatter.45
  3036.2 17.1 reduce-scatter.65
  3055.8 75.0 reduce-scatter.59
  3133.1 77.1 reduce-scatter.37
  3213.1 19.3 reduce-scatter.47
  3235.5 17.1 reduce-scatter.67
  3254.3 44.1 all-gather.33
  3300.4 44.6 all-gather.23
  3348.0 17.6 reduce-scatter.49
  3368.4 17.0 reduce-scatter.69
  3387.7 75.0 reduce-scatter.61
  3465.2 77.1 reduce-scatter.39
  3544.7 135.7 reduce-scatter.63
  3683.3 15.5 reduce-scatter.51
  3701.7 17.1 reduce-scatter.71
  3720.5 44.1 all-gather.35
  3766.7 44.6 all-gather.25
where the time goes:
time: 3860 us; the launch traced here: 3830 us
  waiting for transfers between devices  1720 us (45%)
  other arithmetic  1150 us (30%)
  blocking collectives  416 us (11%)
  local copies, waits for them, and re-layouts  336 us (9%)
  matrix products  174 us (5%)
    while x708, other arithmetic  741 us
    reduce_scatter x1, waiting for transfers between devices, on_device(): lax.psum_scatter(grads[0], ('fsdp', 'ns'), scatter_dimension=0, tiled=True)  362 us
    reduce_scatter x4, waiting for transfers between devices, grams_by_groups(): lax.psum_scatter(partials[0], 'ns', scatter_dimension=0, tiled=True)  309 us
    reduce_scatter x4, waiting for transfers between devices, grams_by_groups(): lax.psum_scatter(partials[3], 'ns', scatter_dimension=0, tiled=True)  257 us
    reduce_scatter x1, waiting for transfers between devices, on_device(): lax.psum_scatter(grads[3], ('fsdp', 'ns'), scatter_dimension=0, tiled=True)  183 us
    all_gather x4, waiting for transfers between devices, grams_by_groups(): lax.all_gather(rounded_shares[0], 'ns', axis=0, tiled=True)  150 us
    unnamed x38, waiting for transfers between devices  149 us
    dynamic_update_slice x128, local copies, waits for them, and re-layouts, block_states(): lax.scan(state_step, start, (jnp.moveaxis(decay, 1, 0), jnp.moveaxis(driv...  138 us
  transfers between devices with their start and end apart: 33, of which 30 were waited for; matrix products, arithmetic and copies ran while one was open for 15% of the time, Pallas kernels for 0%

commit v1 on v0

v1 whole, which is shorter than its diff:
```python
import functools
import math

import jax
import jax.numpy as jnp
from jax import lax
from jax.experimental import pallas as pl
from jax.experimental.pallas import tpu as pltpu
from jax.sharding import PartitionSpec as P

DMODEL = 1024
DINNER = 2048
DSTATE = 16
DTRANK = 64
KCONV = 4
NS_STEPS = 4
STEP_NO = 10


NORM_EPS = 1e-05
FROB_EPS = 1e-07
COEF_A = 3.4445
COEF_B = -4.775
COEF_C = 2.0315
MOMENTUM = 0.95
SHRINK = 0.001
FIRST_MOMENT_BETA = 0.9
BETA_SECOND = 0.95
ADAM_EPS = 1e-08
ADAM_RATE = 1.0
ADAM_DECAY = 0.001


def contract(left, right, left_dim, right_dim):
    return lax.dot_general(
        left, right, (((left_dim,), (right_dim,)), ((), ())), preferred_element_type=jnp.float32
    )


MESH = pl.DeviceIdType.MESH
LANES = 128
SUBS = 8
PASS = LANES * SUBS
STEPS = 4
RESET = 1.0e4
LOG2E = math.log2(math.e)
LN2 = math.log(2.0)
TAPS = DSTATE
CBIAS = TAPS + KCONV
DTBIAS = CBIAS + 1
SKIP = CBIAS + 2
GAIN = CBIAS + 3
VECS = CBIAS + 4
CHUNKS = 16
BAND = 512
SMALL_COLUMNS = 2 * LANES
VEC_AT = LANES + DTRANK


def lane_tile(j):
    return pl.ds(j * LANES, LANES)


def scan_kernel(
    bc_ref,
    proj_ref,
    masks_ref,
    dtw_ref,
    u_ref,
    gate_ref,
    tokens_ref,
    cot_ref,
    outw_ref,
    vec_ref,
    dgate_ref,
    du_ref,
    ddt_ref,
    gsum_ref,
    gamat_ref,
    dbc_ref,
    gout_ref,
    block_ref,
    gated_s,
    amat_s,
    gamat_s,
    pre_s,
    dg_s,
    delta_s,
    dec_s,
    drive_s,
    dstate_s,
    y_s,
    pull_s,
    ddelta_s,
    states,
    prod_a,
    prod_b,
    sums_b,
    sums_c,
):
    length = u_ref.shape[0]
    half = pl.program_id(0)
    bias_row = vec_ref[DTBIAS : DTBIAS + 1, :]

    pre_s[...] = contract(proj_ref[...].astype(jnp.bfloat16), dtw_ref[...], 1, 1) + bias_row
    dg_s[...] = contract(cot_ref[...], outw_ref[...], 1, 1)

    for j in range(SUBS):
        rates = -LOG2E * jnp.exp(vec_ref[0:DSTATE, j * LANES : (j + 1) * LANES])
        amat_s[pl.ds(j, DSTATE, stride=SUBS), :] = rates

    def amat_of(n):
        return amat_s[n * SUBS : (n + 1) * SUBS, :]

    rows = 16

    def prepare(i, carry):
        r = pl.multiple_of(i * rows, rows)
        keep = masks_ref[pl.ds(r, rows), 1:2] > 0.0
        for j in range(SUBS):
            at = (pl.ds(r, rows), lane_tile(j))
            delta = jax.nn.softplus(pre_s[at])
            u = u_ref[at].astype(jnp.float32)
            gate = gate_ref[at]
            delta_s[at] = delta
            to = (pl.ds(r * SUBS + j, rows, stride=SUBS), slice(None))
            dec_s[to] = jnp.where(keep, delta, RESET)
            drive_s[to] = delta * u
            dstate_s[to] = dg_s[at] * (gate * jax.nn.sigmoid(gate))
        return carry

    lax.fori_loop(0, length // rows, prepare, 0)

    for n in range(DSTATE):
        states[n] = jnp.zeros((SUBS, LANES), jnp.float32)

    def tile_of(ref, t):
        return ref[pl.ds(pl.multiple_of(t * SUBS, SUBS), SUBS), :]

    def put_tile(ref, t, value):
        ref[pl.ds(pl.multiple_of(t * SUBS, SUBS), SUBS), :] = value

    def ahead(i, carry):
        state = list(carry)
        for k in range(STEPS):
            t = i * STEPS + k
            dec, drive = tile_of(dec_s, t), tile_of(drive_s, t)
            parts = [None, None]
            for n in range(DSTATE):
                s = jnp.exp2(dec * amat_of(n)) * state[n] + drive * bc_ref[t, DTRANK + n]
                state[n] = s
                states[(t + 1) * DSTATE + n] = s
                term = s * bc_ref[t, DTRANK + DSTATE + n]
                parts[n % 2] = term if parts[n % 2] is None else parts[n % 2] + term
            put_tile(y_s, t, parts[0] + parts[1])
        return tuple(state)

    zero = jnp.zeros((SUBS, LANES), jnp.float32)
    lax.fori_loop(0, length // STEPS, ahead, (zero,) * DSTATE)

    pick = (
        lax.broadcasted_iota(jnp.int32, (2 * DSTATE, 2 * LANES), 1) // SUBS
        == lax.broadcasted_iota(jnp.int32, (2 * DSTATE, 2 * LANES), 0)
    ).astype(jnp.bfloat16)
    span = DSTATE * SUBS

    def channel_sums(products, t0):
        for k in range(0, STEPS, 2):
            block = products[k * span : (k + 2) * span, :]
            row = pl.multiple_of((t0 + k) * DSTATE, 2 * DSTATE)
            both = jnp.dot(pick, block, preferred_element_type=jnp.float32)
            sums_b[pl.ds(row, 2 * DSTATE), :] = both[:, 0:LANES]
            sums_c[pl.ds(row, 2 * DSTATE), :] = both[:, LANES : 2 * LANES]

    def behind_steps(t0, products, flow, g_amat):
        for k in reversed(range(STEPS)):
            t = t0 + k
            dec, drive, dstate = tile_of(dec_s, t), tile_of(drive_s, t), tile_of(dstate_s, t)
            pull, back = [None, None], [None, None]
            pend_b, pend_c = None, None
            for n in range(DSTATE):
                amat = amat_of(n)
                adj = dstate * bc_ref[t, DTRANK + DSTATE + n] + flow[n]
                term = adj * bc_ref[t, DTRANK + n]
                pull[n % 2] = term if pull[n % 2] is None else pull[n % 2] + term
                flow[n] = jnp.exp2(dec * amat) * adj
                weighted = flow[n] * states[t * DSTATE + n]
                g_amat[n] = g_amat[n] + weighted * dec
                term = weighted * amat
                back[n % 2] = term if back[n % 2] is None else back[n % 2] + term
                prod_b_n = adj * drive
                prod_c_n = states[(t + 1) * DSTATE + n] * dstate
                if n % 2:
                    row = k * span + (n - 1) * SUBS
                    products[row : row + 2 * SUBS, 0:LANES] = jnp.concatenate(
                        [pend_b, prod_b_n], axis=0
                    ).astype(jnp.bfloat16)
                    products[row : row + 2 * SUBS, LANES : 2 * LANES] = jnp.concatenate(
                        [pend_c, prod_c_n], axis=0
                    ).astype(jnp.bfloat16)
                pend_b, pend_c = prod_b_n, prod_c_n
            put_tile(pull_s, t, pull[0] + pull[1])
            put_tile(ddelta_s, t, back[0] + back[1])

    groups = length // (2 * STEPS)

    def behind(i, carry):
        flow, g_amat = list(carry[0]), list(carry[1])
        t1 = length - (2 * i + 1) * STEPS
        channel_sums(prod_b, t1 + STEPS)
        behind_steps(t1, prod_a, flow, g_amat)
        channel_sums(prod_a, t1)
        behind_steps(t1 - STEPS, prod_b, flow, g_amat)
        return (tuple(flow), tuple(g_amat))

    unused, g_amat = lax.fori_loop(0, groups, behind, ((zero,) * DSTATE, (zero,) * DSTATE))
    channel_sums(prod_b, 0)
    for n in range(DSTATE):
        gamat_s[n * SUBS : (n + 1) * SUBS, :] = g_amat[n]
    for j in range(SUBS):
        cols = slice(j * LANES, (j + 1) * LANES)
        of_rates = gamat_s[pl.ds(j, DSTATE, stride=SUBS), :]
        gamat_ref[:, cols] = of_rates * -jnp.exp(vec_ref[0:DSTATE, cols])

    line = lax.broadcasted_iota(jnp.int32, (2 * LANES, LANES), 0)
    column = lax.broadcasted_iota(jnp.int32, (2 * LANES, LANES), 1)
    first = line < LANES
    total = jnp.zeros((length, LANES), jnp.float32)
    for n in range(DSTATE):
        goes = jnp.where(first, DTRANK + n, DTRANK + DSTATE + n) == column
        goes = goes.astype(jnp.bfloat16)
        for side, sums in enumerate((sums_b, sums_c)):
            value = sums[pl.ds(n, length, stride=DSTATE), :]
            upper = value.astype(jnp.bfloat16)
            lower = (value - upper.astype(jnp.float32)).astype(jnp.bfloat16)
            part = goes[side * LANES : (side + 1) * LANES, :]
            total = total + jnp.dot(upper, part, preferred_element_type=jnp.float32)
            total = total + jnp.dot(lower, part, preferred_element_type=jnp.float32)

    @pl.when(half == 0)
    def _():
        dbc_ref[...] = total

    @pl.when(half > 0)
    def _():
        dbc_ref[...] += total

    gsum_ref[...] = jnp.zeros_like(gsum_ref)

    def finish(i, carry):
        r = pl.multiple_of(i * rows, rows)
        for j in range(SUBS):
            at = (pl.ds(r, rows), lane_tile(j))
            of = (pl.ds(r * SUBS + j, rows, stride=SUBS), slice(None))
            skip = vec_ref[SKIP : SKIP + 1, j * LANES : (j + 1) * LANES]
            u = u_ref[at].astype(jnp.float32)
            gate = gate_ref[at]
            sig = jax.nn.sigmoid(gate)
            act = gate * sig
            dg = dg_s[at]
            y = y_s[of] + skip * u
            gated_s[at] = (y * act).astype(jnp.bfloat16)
            dgate_ref[at] = (dg * y * sig * (1.0 + gate * (1.0 - sig))).astype(jnp.bfloat16)
            dstate = dg * act
            pull = pull_s[of]
            du_ref[at] = dstate * skip + pull * delta_s[at]
            ddt = (ddelta_s[of] * LN2 + pull * u) * jax.nn.sigmoid(pre_s[at])
            ddt_ref[at] = ddt.astype(jnp.bfloat16)
            cols = slice(j * LANES, (j + 1) * LANES)
            g_skip = dstate * u
            gsum_ref[0:8, cols] += g_skip[0:8] + g_skip[8:16]
            gsum_ref[8:16, cols] += ddt[0:8] + ddt[8:16]
        return carry

    lax.fori_loop(0, length // rows, finish, 0)

    for b in range(0, PASS, BAND):
        strip = slice(b, b + BAND)
        gout_ref[strip, :] = contract(gated_s[:, strip], cot_ref[...], 0, 0).astype(jnp.bfloat16)
    through = jnp.dot(gated_s[...], outw_ref[...], preferred_element_type=jnp.float32)

    @pl.when(half == 0)
    def _():
        block_ref[...] = tokens_ref[...].astype(jnp.float32) + through

    @pl.when(half > 0)
    def _():
        block_ref[...] += through


def scan_both(proj, masks, dt_rows, u_low, gate_in, tokens, cotangent, out_low, vecs):
    length, inner = u_low.shape
    width = out_low.shape[1]
    by_channel = lambda h: (0, h)
    whole = lambda h: (0, 0)
    rows_of = lambda h: (h, 0)
    f32, b16 = jnp.float32, jnp.bfloat16
    return pl.pallas_call(
        scan_kernel,
        grid=(inner // PASS,),
        in_specs=[
            pl.BlockSpec(memory_space=pltpu.SMEM),
            pl.BlockSpec((length, LANES), whole),
            pl.BlockSpec((length, LANES), whole),
            pl.BlockSpec((PASS, LANES), rows_of),
            pl.BlockSpec((length, PASS), by_channel),
            pl.BlockSpec((length, PASS), by_channel),
            pl.BlockSpec((length, width), whole),
            pl.BlockSpec((length, width), whole),
            pl.BlockSpec((PASS, width), rows_of),
            pl.BlockSpec((VECS, PASS), by_channel),
        ],
        out_specs=[
            pl.BlockSpec((length, PASS), by_channel),
            pl.BlockSpec((length, PASS), by_channel),
            pl.BlockSpec((length, PASS), by_channel),
            pl.BlockSpec((16, PASS), by_channel),
            pl.BlockSpec((DSTATE, PASS), by_channel),
            pl.BlockSpec((length, LANES), whole),
            pl.BlockSpec((PASS, width), rows_of),
            pl.BlockSpec((length, width), whole),
        ],
        out_shape=[
            jax.ShapeDtypeStruct((length, inner), b16),
            jax.ShapeDtypeStruct((length, inner), f32),
            jax.ShapeDtypeStruct((length, inner), b16),
            jax.ShapeDtypeStruct((16, inner), f32),
            jax.ShapeDtypeStruct((DSTATE, inner), f32),
            jax.ShapeDtypeStruct((length, LANES), f32),
            jax.ShapeDtypeStruct((inner, width), b16),
            jax.ShapeDtypeStruct((length, width), f32),
        ],
        scratch_shapes=[
            pltpu.VMEM((length, PASS), b16),
            pltpu.VMEM((DSTATE * SUBS, LANES), f32),
            pltpu.VMEM((DSTATE * SUBS, LANES), f32),
        ]
        + [pltpu.VMEM((length, PASS), f32)] * 3
        + [pltpu.VMEM((length * SUBS, LANES), f32)] * 6
        + [
            pltpu.VMEM(((length + 1) * DSTATE, SUBS, LANES), f32),
            pltpu.VMEM((STEPS * DSTATE * SUBS, 2 * LANES), b16),
            pltpu.VMEM((STEPS * DSTATE * SUBS, 2 * LANES), b16),
            pltpu.VMEM(((length + STEPS) * DSTATE, LANES), f32),
            pltpu.VMEM(((length + STEPS) * DSTATE, LANES), f32),
        ],
        compiler_params=pltpu.CompilerParams(vmem_limit_bytes=60 * 1024 * 1024),
        cost_estimate=pl.CostEstimate(
            flops=24 * length * inner * DSTATE,
            bytes_accessed=24 * length * inner,
            transcendentals=2 * length * inner * DSTATE,
        ),
    )(proj, proj, masks, dt_rows, u_low, gate_in, tokens, cotangent, out_low, vecs)


def flipped(index, bit):
    return index + bit * (1 - 2 * lax.rem(lax.div(index, bit), 2))


ROUTES = 3


def each_mask(first, last, body):
    count = abs(last - first)
    sign = 1 if last > first else -1
    if count <= 4:
        for k in range(count):
            body(first + sign * k)
        return

    def step(k, carry):
        body(first + sign * k)
        return carry

    lax.fori_loop(0, count, step, 0)


def routes_of(width, share=4):
    tiles = width // LANES
    last = tiles // share
    counts = ((tiles - last + 1) // 2, (tiles - last) // 2, last)
    firsts = (0, counts[0], counts[0] + counts[1])
    return [(g, firsts[g] * LANES, counts[g] * LANES) for g in range(ROUTES) if counts[g]]


class Cube:
    def __init__(self, fsdp, ns):
        self.fsdp, self.ns = fsdp, ns
        self.shards, self.pieces, self.masks = fsdp * ns, fsdp * ns // 2, fsdp // 2
        order = [2 << k for k in range(fsdp.bit_length() - 2)]
        self.orders = (order, order[:-2] + [order[-1], order[-2]], order)
        self.places = len(order)
        self.row, self.col = lax.axis_index("fsdp"), lax.axis_index("ns")
        self.me = self.row * ns + self.col
        self.sibling = (flipped(self.row, 1), self.col)
        self.sibling_step = (flipped(self.row, 1) - self.row) * ns
        self.core = lax.rem(self.row, 2)
        self.above, self.below = (self.row, self.col + 1), (self.row, self.col - 1)
        self.has_above, self.has_below = self.col < ns - 1, self.col > 0
        self.half_row = lax.div(self.row, 2)
        moves = {bit: flipped(self.row, bit) - self.row for bit in order}
        halves = {bit: flipped(self.half_row, bit // 2) - self.half_row for bit in order}
        self.steps = [[moves[bit] for bit in bits] for bits in self.orders]
        self.half_steps = [[halves[bit] for bit in bits] for bits in self.orders]

    def partner(self, route, place):
        return (self.row + self.steps[route][place], self.col)

    def flips(self, mask, steps, start):
        for place, step in enumerate(steps):
            if isinstance(mask, int):
                start = start + step if mask >> place & 1 else start
            else:
                start = start + lax.rem(lax.div(mask, 1 << place), 2) * step
        return start

    def at(self, mask, col, route):
        return self.flips(mask, self.steps[route], self.row) * self.ns + col

    def spot(self, mask, col, route):
        return self.flips(mask, self.half_steps[route], self.half_row) * self.ns + col

    def wrapped(self, distance):
        col = self.col + distance
        return jnp.where(col < self.ns, col, col - self.ns)

    def greet(self, others=()):
        barrier = pltpu.get_barrier_semaphore()

        def signal(device):
            pl.semaphore_signal(barrier, inc=1, device_id=device, device_id_type=MESH)

        for place in range(self.places):
            signal(self.partner(0, place))
        signal(self.sibling)
        for other in others:
            signal(other)
        pl.when(self.has_above)(lambda: signal(self.above))
        pl.when(self.has_below)(lambda: signal(self.below))
        ends = jnp.where(self.has_above, 1, 0) + jnp.where(self.has_below, 1, 0)
        pl.semaphore_wait(barrier, self.places + 1 + len(others) + ends)

    def along_line(self, distance, step_to):
        pl.when(self.col - distance >= 0)(lambda: step_to(self.col - distance, "above"))
        pl.when(self.col + distance < self.ns)(lambda: step_to(self.col + distance, "below"))

    def upward(self, step, after=None, own=True, between=lambda: None, third=True):
        after = after or (lambda place, k: None)
        nothing, every, both = 0, range(self.places), ("above", "below")
        if own:
            step((0, 1, 2), nothing, self.col, both, every, True)
            after(-1, nothing)

        def along(d, carry):
            self.along_line(
                d, lambda col, way: step((0, 1), nothing, col, (way,), every, False)
            )
            after(-1, d)
            return carry

        lax.fori_loop(1, self.ns, along, 0)
        for place in every if third else ():
            later = range(place + 1, self.places)
            each_mask(
                1 << place,
                2 << place,
                lambda mask: step((2,), mask, self.col, both, later, False),
            )
        done = 1
        for place in every:
            between()
            later = range(place + 1, self.places)

            def of_mask(mask):
                def across(k, carry):
                    step((0, 1), mask, self.wrapped(k), (), later, False)
                    after(place, mask * self.ns + k)
                    return carry

                lax.fori_loop(0, self.ns, across, 0)

            each_mask(1 << place, 2 << place, of_mask)
            until = self.ns if place == self.places - 1 else min(done + 1, self.ns)
            if not third:
                continue

            def last(distance, carry):
                def of_mask(mask):
                    self.along_line(
                        distance, lambda col, way: step((2,), mask, col, (way,), (), False)
                    )

                each_mask(0, self.masks, of_mask)
                return carry

            lax.fori_loop(done, until, last, 0)
            done = until

    def down_stage(self, stage, step, after=None, third=True):
        after = after or (lambda place, k: None)
        nothing, every, both = 0, range(self.places), ("below", "above")
        source = {"above": ("below",), "below": ("above",)}
        if stage > self.places:
            step((0, 1, 2), nothing, self.col, None, both, every)
            return
        if stage == self.places:

            def along(k, carry):
                self.along_line(
                    self.ns - 1 - k,
                    lambda col, way: step((0, 1), nothing, col, other(way), source[other(way)], every),
                )
                after(-1, k)
                return carry

            lax.fori_loop(0, self.ns - 1, along, 0)
            for place in reversed(every if third else ()):
                later = range(place + 1, self.places)
                each_mask(
                    (2 << place) - 1,
                    (1 << place) - 1,
                    lambda mask: step((2,), mask, self.col, place, both, later),
                )
            return
        place = self.places - 1 - stage
        later = range(place + 1, self.places)

        def of_mask(mask):
            def across(i, carry):
                far = jnp.where(2 * self.col < self.ns, self.ns - 1 - i, 1 + i)
                far = jnp.where(far == self.ns, 0, far)
                step((0, 1), mask, self.wrapped(far), place, (), later)
                after(place, ((2 << place) - 1 - mask) * self.ns + i)
                return carry

            lax.fori_loop(0, self.ns, across, 0)

        each_mask((2 << place) - 1, (1 << place) - 1, of_mask)
        first = self.ns - 1 if stage == 0 else 1
        last = 2 if stage == 0 and self.places > 1 else 1

        def line_first(k, carry):
            def of_mask(mask):
                self.along_line(
                    first - k,
                    lambda col, way: step((2,), mask, col, other(way), source[other(way)], ()),
                )

            each_mask(self.masks - 1, -1, of_mask)
            return carry

        if stage < 2 and third:
            lax.fori_loop(0, first - last + 1, line_first, 0)

    def downward(self, step):
        for stage in range(self.places + 2):
            self.down_stage(stage, step)


def other(way):
    return "below" if way == "above" else "above"


def send(src, dst, send_sem, recv_sem, device):
    pltpu.make_async_remote_copy(
        src_ref=src,
        dst_ref=dst,
        send_sem=send_sem,
        recv_sem=recv_sem,
        device_id=device,
        device_id_type=MESH,
    ).start()


def await_bytes(ref, sem):
    pltpu.make_async_copy(ref, ref, sem).wait()


def pass_on(cube, route, mask, col, ways, places, source, target, send_sem, sem_of):
    if "above" in ways:
        pl.when(cube.has_above)(
            lambda: send(source, target, send_sem.at[1], sem_of(mask, col), cube.above)
        )
    if "below" in ways:
        pl.when(cube.has_below)(
            lambda: send(source, target, send_sem.at[2], sem_of(mask, col), cube.below)
        )
    for p in places:
        partner = cube.partner(route, p)
        send(source, target, send_sem.at[0], sem_of(mask + (1 << p), col), partner)


def await_passed(cube, route, ref, send_sem):
    many = cube.masks if route == 2 else 1
    crossed = cube.masks - 1 if route == 2 else cube.pieces - cube.ns
    await_bytes(ref.at[pl.ds(0, crossed)], send_sem.at[0])
    for col in range(cube.ns):

        @pl.when(cube.col == col)
        def _():
            if col + 1 < cube.ns:
                await_bytes(ref.at[pl.ds(0, many * (col + 1))], send_sem.at[1])
            if col:
                await_bytes(ref.at[pl.ds(0, many * (cube.ns - col))], send_sem.at[2])


def gather_step(cube, ins, outs, sems):
    send_sem, recv_sem, pair_send, pair_sem = sems

    def step(routes, mask, col, ways, places, own):
        for a, (mine, out) in enumerate(zip(ins, outs)):
            for route, first, count in routes_of(mine.shape[1]):
                if route not in routes:
                    continue
                cols = pl.ds(first, count)
                block = out.at[cube.at(mask, col, route), :, cols]

                def sem_of(mask, col):
                    return recv_sem.at[a, route, mask, col]

                if not own:
                    await_bytes(block, sem_of(mask, col))
                source = mine.at[:, cols] if own else block
                pass_on(
                    cube, route, mask, col, ways, places, source, block, send_sem.at[a, route], sem_of
                )
                send(source, block, pair_send.at[a], pair_sem.at[a], cube.sibling)

    return step


def own_step(cube, step):
    step((0, 1, 2), 0, cube.col, ("above", "below"), range(cube.places), True)


def front_kernel(
    fsdp,
    ns,
    per_device,
    gains,
    lengths_ref,
    tokens_ref,
    in_ref,
    out_ref,
    x_own,
    dt_own,
    vectors_own,
    gain_own,
    all_in,
    all_out,
    x_rows,
    dt_rows,
    vec_ref,
    gain_ref,
    xpart_far,
    gate_far,
    upre_far,
    u_far,
    proj_ref,
    masks_ref,
    hidden_ref,
    inverse_ref,
    xpart_ref,
    gate_ref,
    upre_ref,
    u_ref,
    away_sem,
    normed_s,
    in_all,
    small_all,
    in_low,
    out_low,
    small_ref,
    small_s,
    x_s,
    dt_s,
    mask_s,
    own_sem,
    send_sem,
    recv_sem,
    pair_send,
    pair_sem,
    send_out,
    recv_out,
    give_out,
    pair_out,
):
    cube = Cube(fsdp, ns)
    length, width = tokens_ref.shape
    in_low[...] = in_ref[...].astype(jnp.bfloat16)
    out_low[...] = out_ref[...].astype(jnp.bfloat16)
    small_s[...] = jnp.zeros_like(small_s)
    small_s[0:per_device, 0 : x_own.shape[1]] = x_own[...]
    small_s[0:per_device, LANES : LANES + dt_own.shape[1]] = dt_own[...]
    small_s[0:DSTATE, VEC_AT : VEC_AT + per_device] = vectors_own[KCONV + 3 :, :]
    small_s[DSTATE:GAIN, VEC_AT : VEC_AT + per_device] = vectors_own[0 : KCONV + 3, :]
    small_s[GAIN:VECS, VEC_AT : VEC_AT + gains] = gain_own[...]
    small_ref[...] = small_s[...].astype(jnp.bfloat16)
    cube.greet()
    first = gather_step(
        cube, (in_low, small_ref), (in_all, small_all), (send_sem, recv_sem, pair_send, pair_sem)
    )
    later = gather_step(cube, (out_low,), (all_out,), (send_out, recv_out, give_out, pair_out))
    own_step(cube, first)
    in_all[cube.me] = in_low[...]
    small_all[cube.me] = small_ref[...]
    own = pltpu.make_async_copy(out_low, all_out.at[cube.me], own_sem.at[0])
    own.start()

    place = lax.broadcasted_iota(jnp.int32, (length, LANES), 0)
    lane = lax.broadcasted_iota(jnp.int32, (length, LANES), 1)
    masks = jnp.ones((length, LANES), jnp.float32)
    for k in range(1, KCONV):
        same = place >= k
        start = jnp.int32(0)
        for d in range(lengths_ref.shape[1]):
            inside = jnp.logical_and(place >= start, place - k < start)
            same = jnp.logical_and(same, jnp.logical_not(inside))
            start = start + lengths_ref[0, d]
        mask_s[k - 1] = jnp.where(same, 1.0, 0.0)
        masks = jnp.where(lane == k, mask_s[k - 1], masks)
    masks_ref[...] = masks

    stage = [0]

    def between():
        stage[0] += 1
        if stage[0] == cube.places:
            own_step(cube, later)

    tokens = tokens_ref[...].astype(jnp.float32)
    inverse = lax.rsqrt(jnp.mean(tokens * tokens, axis=-1, keepdims=True) + NORM_EPS)
    normed_s[...] = tokens * inverse
    inverse_ref[...] = jnp.broadcast_to(inverse, inverse_ref.shape)
    cube.upward(first, own=False, between=between)
    for a, out in enumerate((in_all, small_all)):
        await_bytes(out.at[pl.ds(0, cube.pieces)], pair_sem.at[a])
    keep_in = pltpu.make_async_copy(in_all, all_in, own_sem.at[1])
    keep_in.start()

    def unpack(d, carry):
        at = pl.ds(pl.multiple_of(d * per_device, per_device), per_device)
        x_s[at, :] = small_all[d, 0:per_device, 0:LANES].astype(jnp.float32)
        both = small_all[d, 0:per_device, LANES : 2 * LANES].astype(jnp.float32)
        own_lanes = lax.broadcasted_iota(jnp.int32, both.shape, 1) < DTRANK
        dt_s[at, :] = jnp.where(own_lanes, both, 0.0)
        return carry

    lax.fori_loop(0, cube.shards, unpack, 0)
    x_rows[...] = x_s[...].astype(jnp.bfloat16)
    dt_rows[...] = dt_s[...].astype(jnp.bfloat16)
    for d in range(cube.shards):
        block = small_all[d, 0:32, LANES : 2 * LANES].astype(jnp.float32)[:, DTRANK:]
        vec_ref[:, d * per_device : (d + 1) * per_device] = block[0:VECS, 0:per_device]
        gain_ref[:, d * gains : (d + 1) * gains] = block[GAIN : GAIN + 1, 0:gains]

    hidden_ref[...] = (normed_s[...] * gain_ref[...]).astype(jnp.bfloat16)
    span = 2 * x_s.shape[0] // CHUNKS
    group = cube.shards // CHUNKS

    def mixed_of(chunk, many):
        weights = in_all[pl.ds(chunk * group, many * group)].reshape(many * span, width)
        return contract(hidden_ref[...], weights, 1, 1)

    def x_block(i, carry):
        cols = pl.ds(pl.multiple_of(2 * i * span, 2 * span), 2 * span)
        xpart_ref[:, cols] = mixed_of(2 * i, 2)
        return carry

    lax.fori_loop(0, CHUNKS // 4, x_block, 0)

    def x_chunk(chunk):
        base = pl.multiple_of(chunk * span, span)
        for j in range(span // LANES):
            cols = pl.ds(pl.multiple_of(base + j * LANES, LANES), LANES)
            x = xpart_ref[:, cols]
            upre = vec_ref[CBIAS : CBIAS + 1, cols] + vec_ref[TAPS : TAPS + 1, cols] * x
            for k in range(1, KCONV):
                moved = pltpu.roll(x, k, 0) * mask_s[k - 1]
                upre = upre + vec_ref[TAPS + k : TAPS + k + 1, cols] * moved
            upre_ref[:, cols] = upre
            u_ref[:, cols] = (upre * jax.nn.sigmoid(upre)).astype(jnp.bfloat16)

    def gate_chunk(chunk):
        base = pl.multiple_of((chunk - CHUNKS // 2) * span, span)
        gate_ref[:, pl.ds(base, span)] = mixed_of(chunk, 1)

    away = [
        pltpu.make_async_copy(source, target, away_sem.at[k])
        for k, (source, target) in enumerate(
            ((xpart_ref, xpart_far), (upre_ref, upre_far), (u_ref, u_far), (gate_ref, gate_far))
        )
    ]
    away[0].start()
    seen = [0]

    def halfway():
        seen[0] += 1
        if seen[0] == cube.places:
            away[1].start()
            away[2].start()

    every = cube.pieces // CHUNKS

    def work(place, k):
        run = gate_chunk if place == cube.places - 1 else x_chunk
        if every == 1:
            run(k)
        else:

            @pl.when(lax.rem(k, every) == 0)
            def _():
                run(lax.div(k, every))

    work(-1, jnp.int32(0))
    cube.upward(later, work, own=False, between=halfway)
    away[3].start()
    proj_ref[...] = jnp.dot(u_ref[...], x_rows[...], preferred_element_type=jnp.float32)
    own.wait()
    keep_in.wait()
    for copy in away:
        copy.wait()
    await_bytes(all_out.at[pl.ds(0, cube.pieces)], pair_out.at[0])
    sent = [
        (in_all, send_sem.at[0], pair_send.at[0]),
        (small_all, send_sem.at[1], pair_send.at[1]),
        (all_out, send_out.at[0], give_out.at[0]),
    ]
    for ref, sems, pair in sent:
        await_bytes(ref.at[pl.ds(0, cube.pieces)], pair)
        for route, start, count in routes_of(ref.shape[2]):
            await_passed(cube, route, ref.at[:, :, pl.ds(start, count)], sems.at[route])


def small_rows(per_device):
    return -(-max(per_device, VECS) // 16) * 16


def gather_and_front(lengths, tokens, params, fsdp, ns):
    shards = fsdp * ns
    length, width = tokens.shape
    in_proj, out_proj, x_own, unused, unused, gain = params
    per_device, gains = x_own.shape[0], gain.shape[1]
    inner = per_device * shards
    small = (small_rows(per_device), SMALL_COLUMNS)
    f32, b16 = jnp.float32, jnp.bfloat16
    held = pl.BlockSpec(memory_space=pltpu.VMEM)
    far = pl.BlockSpec(memory_space=pl.ANY)

    def shape(*dims, dtype=f32):
        return jax.ShapeDtypeStruct(dims, dtype)

    return pl.pallas_call(
        functools.partial(front_kernel, fsdp, ns, per_device, gains),
        in_specs=[pl.BlockSpec(memory_space=pltpu.SMEM)] + [held] * 7,
        out_specs=[far] * 2 + [held] * 4 + [far] * 4 + [held] * 4,
        out_shape=[
            shape(shards, *in_proj.shape, dtype=b16),
            shape(shards, *out_proj.shape, dtype=b16),
            shape(inner, LANES, dtype=b16),
            shape(inner, LANES, dtype=b16),
            shape(VECS, inner),
            shape(1, width),
            shape(length, inner),
            shape(length, inner),
            shape(length, inner),
            shape(length, inner, dtype=b16),
            shape(length, LANES),
            shape(length, LANES),
            shape(length, width, dtype=b16),
            shape(length, LANES),
        ],
        scratch_shapes=[
            pltpu.VMEM((length, inner), f32),
            pltpu.VMEM((length, inner), f32),
            pltpu.VMEM((length, inner), f32),
            pltpu.VMEM((length, inner), b16),
            pltpu.SemaphoreType.DMA((4,)),
            pltpu.VMEM((length, width), f32),
            pltpu.VMEM((shards,) + in_proj.shape, b16),
            pltpu.VMEM((shards,) + small, b16),
            pltpu.VMEM(in_proj.shape, b16),
            pltpu.VMEM(out_proj.shape, b16),
            pltpu.VMEM(small, b16),
            pltpu.VMEM(small, f32),
            pltpu.VMEM((inner, LANES), f32),
            pltpu.VMEM((inner, LANES), f32),
            pltpu.VMEM((KCONV - 1, length, LANES), f32),
            pltpu.SemaphoreType.DMA((2,)),
            pltpu.SemaphoreType.DMA((2, ROUTES, 3)),
            pltpu.SemaphoreType.DMA((2, ROUTES, fsdp // 2, ns)),
            pltpu.SemaphoreType.DMA((2,)),
            pltpu.SemaphoreType.DMA((2,)),
            pltpu.SemaphoreType.DMA((1, ROUTES, 3)),
            pltpu.SemaphoreType.DMA((1, ROUTES, fsdp // 2, ns)),
            pltpu.SemaphoreType.DMA((1,)),
            pltpu.SemaphoreType.DMA((1,)),
        ],
        compiler_params=pltpu.CompilerParams(
            collective_id=0, has_side_effects=True, vmem_limit_bytes=56 * 1024 * 1024
        ),
    )(lengths, tokens, *params)


def slots_of(cube, route):
    if route == 2:

        def over(mask, col):
            if isinstance(mask, int):
                return (2 * cube.masks + mask // cube.ns, mask % cube.ns)
            return (2 * cube.masks + lax.div(mask, cube.ns), lax.rem(mask, cube.ns))

        below = lambda mask, col: (mask, col)
        above = lambda mask, col: (cube.masks + mask, col)
        return (below, above, over, cube.masks)
    return (
        lambda mask, col: (0, col),
        lambda mask, col: (1, col),
        lambda mask, col: (mask + 1, col),
        1,
    )


def slot_count(fsdp, ns, route):
    masks = fsdp // 2
    return 2 * masks + -(-masks // ns) if route == 2 else masks + 1


def clear_ends(cube, route, land):
    many = slots_of(cube, route)[3]

    def clear(first):
        ref = land.at[pl.ds(first, many)]
        ref[...] = jnp.zeros_like(ref)

    pl.when(jnp.logical_not(cube.has_below))(lambda: clear(0))
    pl.when(jnp.logical_not(cube.has_above))(lambda: clear(many))


def arrivals(cube, route, mask, col, lines, places, wait):
    below, above, over, unused = slots_of(cube, route)
    slots = [over(mask + (1 << p), col) for p in places]
    for slot in slots:
        wait(slot)
    if "below" in lines:
        pl.when(cube.has_below)(lambda: wait(below(mask, col)))
        slots.append(below(mask, col))
    if "above" in lines:
        pl.when(cube.has_above)(lambda: wait(above(mask, col)))
        slots.append(above(mask, col))
    return slots


def hand_on(cube, route, mask, col, to, give):
    below, above, over, unused = slots_of(cube, route)
    if to == "above":
        give(below(mask, col), cube.above)
    elif to == "below":
        give(above(mask, col), cube.below)
    elif to is not None:
        give(over(mask, col), cube.partner(route, to))


def scatter_steps(cube, parts, sums, pairs, lands, sems):
    send_sem, recv_sem, pair_sem = sems

    def pieces(routes):
        for a, part in enumerate(parts):
            for k, (route, first, count) in enumerate(routes_of(part.shape[2])):
                if route in routes:
                    yield (a, route, pl.ds(first, count), pairs[a][k], lands[a][k])

    def give_pair(routes, mask, col, to, lines, places):
        for a, route, cols, pair, unused in pieces(routes):
            index = cube.at(mask, col, route) + cube.sibling_step
            send(
                parts[a].at[index, :, cols],
                pair.at[mask, col],
                send_sem.at[a],
                pair_sem.at[a, route, mask, col],
                cube.sibling,
            )

    def step(routes, mask, col, to, lines, places):
        for a, route, cols, pair, land in pieces(routes):
            index = cube.at(mask, col, route)
            rows = parts[a].shape[1]
            await_bytes(pair.at[mask, col], pair_sem.at[a, route, mask, col])

            def wait(slot):
                await_bytes(land.at[slot], recv_sem.at[(a, route) + slot])

            slots = arrivals(cube, route, mask, col, lines, places, wait)
            deep = min(rows, 16)
            for r in range(0, rows, deep):
                at = pl.ds(r, deep)
                total = parts[a][index, at, cols].astype(jnp.float32)
                total = total + pair[mask, col, at, :].astype(jnp.float32)
                for slot in slots:
                    total = total + land[slot + (at, slice(None))].astype(jnp.float32)
                if to is not None:
                    pair[mask, col, at, :] = total.astype(jnp.bfloat16)
                else:
                    sums[a][at, cols] = total

            def give(slot, device):
                send(
                    pair.at[mask, col],
                    land.at[slot],
                    send_sem.at[a],
                    recv_sem.at[(a, route) + slot],
                    device,
                )

            hand_on(cube, route, mask, col, to, give)

    return (give_pair, step)


def back_kernel(
    fsdp,
    ns,
    per_device,
    far,
    inverse_ref,
    masks_ref,
    proj_ref,
    x_rows,
    dt_rows,
    vec_ref,
    gain_ref,
    gsum_ref,
    gamat_ref,
    dbc_ref,
    all_in,
    dtok_ref,
    ggain_ref,
    sum_in,
    sum_out,
    sum_small,
    sum_vec,
    near,
    near_sem,
    part_in,
    part_small,
    small_s,
    pair_in,
    pair_out,
    pair_small,
    land_in,
    land_out,
    land_small,
    dx_s,
    dhidden_s,
    weights,
    mask_s,
    dproj_s,
    dtin_s,
    du_s,
    gx_s,
    gdt_s,
    last_s,
    load_sem,
    send_first,
    recv_first,
    pair_first,
    send_sem,
    recv_sem,
    pair_sem,
):
    copies = [
        pltpu.make_async_copy(source, target, near_sem.at[k])
        for k, (source, target) in enumerate(zip(far, near))
    ]
    for copy in copies:
        copy.start()
    (
        gout_ref,
        dgate_ref,
        hidden_ref,
        ddt_ref,
        du_ref,
        u_ref,
        upre_ref,
        xpart_ref,
        tokens_ref,
        cot_ref,
    ) = near
    cube = Cube(fsdp, ns)
    length, width = tokens_ref.shape
    inner = x_rows.shape[0]
    cube.greet()
    give_out, step_out = scatter_steps(
        cube, (gout_ref,), (sum_out,), (pair_out,), (land_out,), (send_first, recv_first, pair_first)
    )
    give_in, step_in = scatter_steps(
        cube,
        (part_in, part_small),
        (sum_in, sum_small),
        (pair_in, pair_small),
        (land_in, land_small),
        (send_sem, recv_sem, pair_sem),
    )
    copies[0].wait()
    cube.downward(give_out)
    for part, land in ((gout_ref, land_out), (part_in, land_in), (part_small, land_small)):
        for (route, unused, unused), where in zip(routes_of(part.shape[2]), land):
            clear_ends(cube, route, where)

    group = BAND // part_in.shape[1]

    def into_part(first, source):
        def band(i, carry):
            cols = pl.ds(pl.multiple_of(i * BAND, BAND), BAND)
            gradient = contract(source[:, cols], hidden_ref[...], 0, 0).astype(jnp.bfloat16)
            at = pl.ds(first + i * group, group)
            part_in[at] = gradient.reshape(group, part_in.shape[1], width)
            return carry

        lax.fori_loop(0, inner // BAND, band, 0)

    for copy in copies[1:3]:
        copy.wait()
    into_part(cube.shards // 2, dgate_ref)
    for k in range(1, KCONV):
        mask_s[k - 1] = jnp.broadcast_to(masks_ref[:, k : k + 1], (length, LANES))
    for copy in copies[3:]:
        copy.wait()
    d_dtin = jnp.dot(ddt_ref[...], dt_rows[...], preferred_element_type=jnp.float32)
    dproj_s[...] = (d_dtin + dbc_ref[...]).astype(jnp.bfloat16)
    lane = lax.broadcasted_iota(jnp.int32, (length, LANES), 1)
    dtin_s[...] = jnp.where(lane < DTRANK, proj_ref[...], 0.0).astype(jnp.bfloat16)
    sub = lax.broadcasted_iota(jnp.int32, (SUBS, LANES), 0)

    def state_band(i, carry):
        at = pl.ds(pl.multiple_of(i * BAND, BAND), BAND)
        du_s[:, at] = du_ref[:, at] + contract(dproj_s[...], x_rows[at, :], 1, 1)
        gx_s[at, :] = contract(u_ref[:, at], dproj_s[...], 0, 0)
        gdt_s[at, :] = contract(ddt_ref[:, at], dtin_s[...], 0, 0)
        return carry

    lax.fori_loop(0, inner // BAND, state_band, 0)

    def x_chunk(chunk):
        cols = pl.ds(pl.multiple_of(chunk * LANES, LANES), LANES)
        x, upre = xpart_ref[:, cols], upre_ref[:, cols]
        sig = jax.nn.sigmoid(upre)
        dpre = du_s[:, cols] * sig * (1.0 + upre * (1.0 - sig))
        dx = vec_ref[TAPS : TAPS + 1, cols] * dpre
        sums = [jnp.sum(dpre * x, axis=0, keepdims=True)]
        for k in range(1, KCONV):
            masked = mask_s[k - 1] * dpre
            dx = dx + vec_ref[TAPS + k : TAPS + k + 1, cols] * pltpu.roll(masked, length - k, 0)
            sums.append(jnp.sum(masked * pltpu.roll(x, k, 0), axis=0, keepdims=True))
        sums.append(jnp.sum(dpre, axis=0, keepdims=True))
        sums.append(jnp.sum(gsum_ref[SUBS : 2 * SUBS, cols], axis=0, keepdims=True))
        sums.append(jnp.sum(gsum_ref[0:SUBS, cols], axis=0, keepdims=True))
        last = jnp.zeros((SUBS, LANES), jnp.float32)
        for k, value in enumerate(sums):
            last = jnp.where(sub == k, value, last)
        last_s[:, cols] = last
        dx_s[:, cols] = dx.astype(jnp.bfloat16)

    steps = ns << (cube.places - 1)
    many = max(CHUNKS // steps, 1)
    every = max(steps // CHUNKS, 1)

    def x_chunks(place, k):
        def run():
            for i in range(many):
                x_chunk((k if every == 1 else lax.div(k, every)) * many + i)

        if every == 1:
            run()
        else:
            pl.when(lax.rem(k, every) == 0)(run)

    cube.down_stage(0, step_out, x_chunks)
    into_part(0, dx_s)

    small_s[...] = jnp.zeros_like(small_s)
    owners = LANES // per_device

    def small_chunk(chunk, carry):
        cols = pl.ds(pl.multiple_of(chunk * LANES, LANES), LANES)
        shape = (owners, per_device, LANES)
        small_s[:, 0:per_device, 0:LANES] = gx_s[cols, :].reshape(shape)
        small_s[:, 0:per_device, LANES:VEC_AT] = gdt_s[cols, :].reshape(shape)[:, :, 0:DTRANK]
        rates, last = gamat_ref[:, cols], last_s[:, cols]
        for o in range(owners):
            mine = slice(o * per_device, (o + 1) * per_device)
            small_s[o, 0:DSTATE, VEC_AT : VEC_AT + per_device] = rates[:, mine]
            small_s[o, DSTATE:VECS, VEC_AT : VEC_AT + per_device] = last[:, mine]
        part_small[pl.ds(chunk * owners, owners)] = small_s[...].astype(jnp.bfloat16)
        return carry

    lax.fori_loop(0, inner // LANES, small_chunk, 0)
    cube.downward(give_in)

    share = cube.shards // CHUNKS
    span = 2 * inner // CHUNKS

    def load(chunk):
        slot = lax.rem(chunk, 2)
        return pltpu.make_async_copy(
            all_in.at[pl.ds(chunk * share, share)], weights.at[slot], load_sem.at[slot]
        )

    dhidden_s[...] = jnp.zeros_like(dhidden_s)
    load(jnp.int32(0)).start()

    def hidden_chunk(chunk, left, base):
        load(chunk).wait()
        pl.when(chunk + 1 < CHUNKS)(lambda: load(chunk + 1).start())
        cols = pl.ds(pl.multiple_of((chunk - base) * span, span), span)
        right = weights[lax.rem(chunk, 2)].reshape(span, width)
        dhidden_s[...] += jnp.dot(left[:, cols], right, preferred_element_type=jnp.float32)

    def tokens_rows(i, total):
        at = pl.ds(pl.multiple_of(i * 16, 16), 16)
        inverse = inverse_ref[at, 0:1]
        normed = tokens_ref[at, :].astype(jnp.float32) * inverse
        dhidden = dhidden_s[at, :]
        product = dhidden * normed
        scaled = dhidden * gain_ref[...]
        mean = jnp.mean(scaled * normed, axis=-1, keepdims=True)
        dtok_ref[at, :] = cot_ref[at, :].astype(jnp.float32) + inverse * (scaled - normed * mean)
        return total + product[0:8] + product[8:16]

    part = CHUNKS // 2

    def hidden_chunks(first, last, left, base):
        def body(chunk, carry):
            hidden_chunk(chunk, left, base)
            return carry

        lax.fori_loop(first, last, body, 0)

    for stage in range(cube.places + 2):
        if stage < cube.places + 1:
            cube.down_stage(stage + 1, step_out)
        cube.down_stage(stage, step_in)
        if stage == 0:
            hidden_chunks(0, part, dx_s, 0)
        if stage == 1:
            hidden_chunks(part, CHUNKS, dgate_ref, part)
        if stage == cube.places:
            zero = jnp.zeros((SUBS, width), jnp.float32)
            total = lax.fori_loop(0, length // 16, tokens_rows, zero)
            row = jnp.sum(total, axis=0, keepdims=True)
            ggain_ref[...] = jnp.zeros_like(ggain_ref)
            for k in range(width // LANES):
                ggain_ref[k : k + 1, :] = row[:, k * LANES : (k + 1) * LANES]
    vectors = sum_small[0:VECS, VEC_AT : VEC_AT + per_device]
    sum_vec[0 : KCONV + 3, :] = vectors[DSTATE:GAIN, :]
    sum_vec[KCONV + 3 :, :] = vectors[0:DSTATE, :]
    await_bytes(gout_ref.at[pl.ds(0, cube.shards - 1)], send_first.at[0])
    await_bytes(part_in.at[pl.ds(0, cube.shards - 1)], send_sem.at[0])
    await_bytes(part_small.at[pl.ds(0, cube.shards - 1)], send_sem.at[1])


def back_and_scatter(far, arrays, all_in, per_device, small, fsdp, ns):
    length, width = arrays[0].shape[0], all_in.shape[2]
    inner = per_device * fsdp * ns
    shards, masks = fsdp * ns, fsdp // 2
    f32, b16 = jnp.float32, jnp.bfloat16
    blocks = [(2 * per_device, width), (per_device, width), (small, SMALL_COLUMNS)]

    def inbox(slots):
        return [
            [
                pltpu.VMEM((slots(route), ns, rows, count), b16)
                for route, unused, count in routes_of(columns)
            ]
            for rows, columns in blocks
        ]

    most = slot_count(fsdp, ns, 2)
    return pl.pallas_call(
        functools.partial(back_kernel, fsdp, ns, per_device),
        in_specs=[
            [pl.BlockSpec(memory_space=pl.ANY)] * len(far),
            *[pl.BlockSpec(memory_space=pltpu.VMEM)] * len(arrays),
            pl.BlockSpec(memory_space=pl.ANY),
        ],
        out_specs=[pl.BlockSpec(memory_space=pltpu.VMEM)] * 6,
        out_shape=[
            jax.ShapeDtypeStruct((length, width), f32),
            jax.ShapeDtypeStruct((-(-width // LANES // 16) * 16, LANES), f32),
        ]
        + [jax.ShapeDtypeStruct(block, f32) for block in blocks]
        + [jax.ShapeDtypeStruct((GAIN, per_device), f32)],
        scratch_shapes=[
            [pltpu.VMEM(array.shape, array.dtype) for array in far],
            pltpu.SemaphoreType.DMA((len(far),)),
            pltpu.VMEM((shards,) + blocks[0], b16),
            pltpu.VMEM((shards,) + blocks[2], b16),
            pltpu.VMEM((LANES // per_device,) + blocks[2], f32),
        ]
        + inbox(lambda route: masks)
        + inbox(functools.partial(slot_count, fsdp, ns))
        + [
            pltpu.VMEM((length, inner), b16),
            pltpu.VMEM((length, width), f32),
            pltpu.VMEM((2, shards // CHUNKS) + blocks[0], b16),
            pltpu.VMEM((KCONV - 1, length, LANES), f32),
            pltpu.VMEM((length, LANES), b16),
            pltpu.VMEM((length, LANES), b16),
            pltpu.VMEM((length, inner), f32),
            pltpu.VMEM((inner, LANES), f32),
            pltpu.VMEM((inner, LANES), f32),
            pltpu.VMEM((SUBS, inner), f32),
            pltpu.SemaphoreType.DMA((2,)),
            pltpu.SemaphoreType.DMA((1,)),
            pltpu.SemaphoreType.DMA((1, ROUTES, most, ns)),
            pltpu.SemaphoreType.DMA((1, ROUTES, masks, ns)),
            pltpu.SemaphoreType.DMA((2,)),
            pltpu.SemaphoreType.DMA((2, ROUTES, most, ns)),
            pltpu.SemaphoreType.DMA((2, ROUTES, masks, ns)),
        ],
        compiler_params=pltpu.CompilerParams(
            collective_id=1, has_side_effects=True, vmem_limit_bytes=60 * 1024 * 1024
        ),
    )(far, *arrays, all_in)


def halves_of(deep, wide):
    if deep >= 32:
        return [(g, (g * (deep // 2), deep // 2), (0, wide)) for g in range(2)]
    return [(g, (0, deep), (first, count)) for g, first, count in routes_of(wide, wide)]


def muon_kernel(
    fsdp,
    ns,
    starts,
    sum_in,
    sum_out,
    in_moment,
    out_moment,
    low_ref,
    gain_ref,
    x_out,
    low_out,
    gain_out,
    rows_s,
    turn,
    back_s,
    mine,
    outbox,
    lands,
    pieces_s,
    gram,
    now,
    poly,
    small_now,
    small_land,
    small_gram,
    low_s,
    send_sem,
    gather_sem,
    recv_sem,
    came_sem,
    swap_sem,
    small_send,
    small_recv,
):
    cube = Cube(fsdp, ns)
    pieces, deep, wide = pieces_s.shape
    width = now.shape[0]
    rows = sum_in.shape[0]
    blocks = width // LANES
    each = LANES // deep
    split = halves_of(deep, wide)
    ways = [cube.sibling] + [cube.partner(0, place) for place in range(cube.places)]
    ways += [(cube.row, flipped(cube.col, 1 << k)) for k in range(ns.bit_length() - 1)]
    stages = len(ways)
    cube.greet(ways[cube.places + 2 :])

    short = sum_out.shape[0]
    rows_s[0] = (MOMENTUM * in_moment[...] + sum_in[...]).astype(jnp.bfloat16)
    rows_s[1, 0:short, :] = (MOMENTUM * out_moment[...] + sum_out[...]).astype(jnp.bfloat16)
    rows_s[1, short:, :] = jnp.zeros((rows - short, width), jnp.bfloat16)

    def swap(source, target, which):
        return pltpu.make_async_remote_copy(
            src_ref=source,
            dst_ref=target,
            send_sem=swap_sem.at[which, 0],
            recv_sem=swap_sem.at[which, 1],
            device_id=cube.sibling,
            device_id_type=MESH,
        )

    there = swap(rows_s.at[1 - cube.core], turn.at[pl.ds(rows, rows)], 0)
    there.start()
    turn[0:rows] = rows_s[cube.core]

    def small_copy(k):
        return pltpu.make_async_remote_copy(
            src_ref=small_now.at[k],
            dst_ref=small_land.at[k],
            send_sem=small_send.at[k],
            recv_sem=small_recv.at[k],
            device_id=ways[k],
            device_id_type=MESH,
        )

    def inverse(total):
        return 1.0 / (jnp.sqrt(jnp.full((1, 1), total, jnp.float32)) + FROB_EPS)

    def diagonal(block):
        on = lax.broadcasted_iota(jnp.int32, block.shape, 0) == lax.broadcasted_iota(
            jnp.int32, block.shape, 1
        )
        return jnp.sum(jnp.where(on, block, 0.0))

    def small_step(k):
        small_copy(k).wait()
        total = small_now[k].astype(jnp.float32) + small_land[k].astype(jnp.float32)
        if k + 1 < stages:
            small_now[k + 1] = total.astype(jnp.bfloat16)
            small_copy(k + 1).start()
            return
        gain_out[...] = total[starts[2] :]
        for which in range(2):
            deep = starts[which + 1] - starts[which]
            whole = jnp.pad(total[starts[which] : starts[which + 1]], ((0, LANES - deep), (0, 0)))
            scale = inverse(diagonal(whole))
            small_gram[which] = whole * (scale * scale)
            low_s[which] = (low_ref[which] * scale).astype(jnp.bfloat16)

    for which in range(2):
        low = low_ref[which].astype(jnp.bfloat16)
        term = contract(low, low, 0, 0)[0 : starts[which + 1] - starts[which]]
        small_now[0, starts[which] : starts[which + 1], :] = term.astype(jnp.bfloat16)
    small_now[0, starts[2] :, :] = gain_ref[...].astype(jnp.bfloat16)
    small_copy(0).start()
    left = list(range(stages))

    def between():
        if left:
            small_step(left.pop(0))

    for (route, unused, unused), land in zip(split, lands):
        clear_ends(cube, route, land)

    there.wait()
    for b in range(blocks):
        if b % 2 == 0:
            band = contract(turn[:, b * LANES : (b + 2) * LANES], turn[...], 0, 0)
        block = band[b % 2 * LANES : (b % 2 + 1) * LANES]
        for c in range(wide // LANES):
            at = (b + c) % blocks * LANES
            for r in range(each):
                strip = block[r * deep : (r + 1) * deep, at : at + LANES]
                mine[b * each + r, :, c * LANES : (c + 1) * LANES] = strip

    def step(routes, mask, col, to, lines, places):
        for (route, rows_at, cols_at), land in zip(split, lands):
            if route not in routes:
                continue
            at = (cube.spot(mask, col, route), pl.ds(*rows_at), pl.ds(*cols_at))

            def wait(slot):
                await_bytes(land.at[slot], recv_sem.at[(route,) + slot])

            total = mine[at]
            for slot in arrivals(cube, route, mask, col, lines, places, wait):
                total = total + land[slot].astype(jnp.float32)
            if to is not None:
                outbox[at] = total.astype(jnp.bfloat16)
            else:
                pieces_s[at] = total.astype(jnp.bfloat16)

            def give(slot, device):
                send(
                    outbox.at[at],
                    land.at[slot],
                    send_sem,
                    recv_sem.at[(route,) + slot],
                    device,
                )

            hand_on(cube, route, mask, col, to, give)

    for stage in range(cube.places + 2):
        cube.down_stage(stage, step, third=False)
        if stage <= cube.places:
            between()

    def spread(routes, mask, col, ways, places, own):
        for route, rows_at, cols_at in split:
            if route not in routes:
                continue
            block = pieces_s.at[cube.spot(mask, col, route), pl.ds(*rows_at), pl.ds(*cols_at)]

            def sem_of(mask, col):
                return came_sem.at[route, mask, col]

            if not own:
                await_bytes(block, sem_of(mask, col))
            sems = gather_sem.at[route]
            pass_on(cube, route, mask, col, ways, places, block, block, sems, sem_of)

    def small_newton():
        for which in range(2):
            whole = small_gram[which]
            low = whole.astype(jnp.bfloat16)
            power = jnp.dot(low, low, preferred_element_type=jnp.float32)
            mixed = (COEF_B * whole + COEF_C * power).astype(jnp.bfloat16)
            block = low_s[which]
            low_s[which] = (
                COEF_A * block.astype(jnp.float32)
                + jnp.dot(block, mixed, preferred_element_type=jnp.float32)
            ).astype(jnp.bfloat16)
            half = COEF_A * whole + jnp.dot(low, mixed, preferred_element_type=jnp.float32)
            small_gram[which] = COEF_A * half + jnp.dot(
                half.astype(jnp.bfloat16), mixed, preferred_element_type=jnp.float32
            )

    def after(place, k):
        if place == cube.places - 1:
            pl.when(k - (ns << place) < NS_STEPS)(small_newton)

    cube.upward(spread, after=after, between=between, third=False)
    low_out[...] = low_s[...]

    for b in range(blocks):
        for c in range(wide // LANES):
            at = (b + c) % blocks * LANES
            for r in range(each):
                now[b * LANES + r * deep : b * LANES + (r + 1) * deep, at : at + LANES] = pieces_s[
                    b * each + r, :, c * LANES : (c + 1) * LANES
                ]
    for b in range(blocks):
        for c in range(wide // LANES, blocks):
            other = (b + c) % blocks
            block = now[other * LANES : (other + 1) * LANES, b * LANES : (b + 1) * LANES]
            flip = block.astype(jnp.float32).T.astype(jnp.bfloat16)
            now[b * LANES : (b + 1) * LANES, other * LANES : (other + 1) * LANES] = flip

    total = jnp.zeros((), jnp.float32)
    for b in range(0, width, LANES):
        total = total + diagonal(now[b : b + LANES, b : b + LANES].astype(jnp.float32))
    factor = inverse(total)
    square = factor * factor
    strip = min(BAND, width)

    def turned(block, k):
        moved = COEF_A * block.astype(jnp.float32) + jnp.dot(
            block, poly[...], preferred_element_type=jnp.float32
        )
        if k == 0:
            moved = moved * factor
        return moved.astype(jnp.bfloat16)

    for k in range(NS_STEPS):

        def poly_strip(i, carry, k=k):
            at = pl.ds(pl.multiple_of(i * strip, strip), strip)
            low = now[at, :]
            power = jnp.dot(low, now[...], preferred_element_type=jnp.float32)
            if k == 0:
                mixed = COEF_B * square * low.astype(jnp.float32) + (COEF_C * square * square) * power
            else:
                mixed = COEF_B * gram[at, :] + COEF_C * power
            poly[at, :] = mixed.astype(jnp.bfloat16)
            return carry

        lax.fori_loop(0, width // strip, poly_strip, 0)
        if k + 1 == NS_STEPS:
            break
        turn[...] = turned(turn[...], k)

        def gram_strip(i, carry, k=k):
            at = pl.ds(pl.multiple_of(i * strip, strip), strip)
            low = now[at, :]
            full = low.astype(jnp.float32) if k == 0 else gram[at, :]
            half = COEF_A * full + jnp.dot(low, poly[...], preferred_element_type=jnp.float32)
            if k == 0:
                half = half * square
            renewed = COEF_A * half + jnp.dot(
                half.astype(jnp.bfloat16), poly[...], preferred_element_type=jnp.float32
            )
            gram[at, :] = renewed
            now[at, :] = renewed.astype(jnp.bfloat16)
            return carry

        lax.fori_loop(0, width // strip, gram_strip, 0)
    turn[rows:] = turned(turn[rows:], NS_STEPS - 1)
    home = swap(turn.at[pl.ds(rows, rows)], back_s, 1)
    home.start()
    x_out[cube.core] = turned(turn[0:rows], NS_STEPS - 1)
    home.wait()
    x_out[1 - cube.core] = back_s[...]
    await_bytes(outbox.at[pl.ds(0, pieces - 1)], send_sem)
    for route, rows_at, cols_at in split:
        sent = pieces_s.at[:, pl.ds(*rows_at), pl.ds(*cols_at)]
        await_passed(cube, route, sent, gather_sem.at[route])


def muon_rows(sum_in, sum_out, in_moment, out_moment, low, columns, gain, fsdp, ns):
    pieces = fsdp * ns // 2
    rows, width = sum_in.shape
    wide = (width // LANES // 2 + 1) * LANES
    deep = width // pieces
    block = (pieces, deep, wide)
    stages = (fsdp * ns).bit_length() - 1
    starts = (0, columns[0], sum(columns))
    small = (sum(columns) + gain.shape[0], LANES)
    f32, b16 = jnp.float32, jnp.bfloat16
    landing = [
        pltpu.VMEM((slot_count(fsdp, ns, route), ns, rows_at[1], cols_at[1]), b16)
        for route, rows_at, cols_at in halves_of(deep, wide)
    ]
    held = pl.BlockSpec(memory_space=pltpu.VMEM)
    return pl.pallas_call(
        functools.partial(muon_kernel, fsdp, ns, starts),
        in_specs=[held] * 6,
        out_specs=[held] * 3,
        out_shape=[
            jax.ShapeDtypeStruct((2, rows, width), b16),
            jax.ShapeDtypeStruct(low.shape, b16),
            jax.ShapeDtypeStruct(gain.shape, f32),
        ],
        scratch_shapes=[
            pltpu.VMEM((2, rows, width), b16),
            pltpu.VMEM((2 * rows, width), b16),
            pltpu.VMEM((rows, width), b16),
            pltpu.VMEM(block, f32),
            pltpu.VMEM(block, b16),
        ]
        + [
            landing,
            pltpu.VMEM(block, b16),
            pltpu.VMEM((width, width), f32),
            pltpu.VMEM((width, width), b16),
            pltpu.VMEM((width, width), b16),
            pltpu.VMEM((stages,) + small, b16),
            pltpu.VMEM((stages,) + small, b16),
            pltpu.VMEM((2, LANES, LANES), f32),
            pltpu.VMEM(low.shape, b16),
            pltpu.SemaphoreType.DMA,
            pltpu.SemaphoreType.DMA((ROUTES, 3)),
            pltpu.SemaphoreType.DMA((ROUTES, slot_count(fsdp, ns, 2), ns)),
            pltpu.SemaphoreType.DMA((ROUTES, fsdp // 2, ns)),
            pltpu.SemaphoreType.DMA((2, 2)),
            pltpu.SemaphoreType.DMA((stages,)),
            pltpu.SemaphoreType.DMA((stages,)),
        ],
        compiler_params=pltpu.CompilerParams(
            collective_id=2, has_side_effects=True, vmem_limit_bytes=48 * 1024 * 1024
        ),
    )(sum_in, sum_out, in_moment, out_moment, low, gain)


def layer(tokens, out_grad, lengths, params, fsdp, ns):
    flat_low, grad_flat = tokens[0], out_grad[0]
    length, width = flat_low.shape
    (
        all_in,
        all_out,
        x_rows,
        dt_rows,
        vecs,
        gain,
        x_part,
        gate_in,
        conv_flat,
        u_low,
        proj,
        masks,
        hidden,
        inverse,
    ) = gather_and_front(lengths, flat_low, params, fsdp, ns)
    per_device = params[2].shape[0]
    inner = x_rows.shape[0]
    out_low = all_out.reshape(inner, width)
    d_gate, d_u, d_dtlow, vec_parts, grad_amat, d_bc, grad_out, block_out = scan_both(
        proj, masks, dt_rows, u_low, gate_in, flat_low, grad_flat, out_low, vecs
    )
    d_tokens, grad_gain, sum_in, sum_out, sum_small, sum_vec = back_and_scatter(
        [
            grad_out.reshape(fsdp * ns, per_device, width),
            d_gate,
            hidden,
            d_dtlow,
            d_u,
            u_low,
            conv_flat,
            x_part,
            flat_low,
            grad_flat,
        ],
        (inverse, masks, proj, x_rows, dt_rows, vecs, gain, vec_parts, grad_amat, d_bc),
        all_in,
        per_device,
        small_rows(per_device),
        fsdp,
        ns,
    )
    return (block_out[None], d_tokens[None], grad_gain, sum_in, sum_out, sum_small, sum_vec)


def adamw_update(param, first, second, grad):
    first_new = FIRST_MOMENT_BETA * first + (1.0 - FIRST_MOMENT_BETA) * grad
    second_new = BETA_SECOND * second + (1.0 - BETA_SECOND) * grad * grad
    first_hat = first_new / (1.0 - FIRST_MOMENT_BETA**STEP_NO)
    second_hat = second_new / (1.0 - BETA_SECOND**STEP_NO)
    param_new = param * (1.0 - ADAM_RATE * ADAM_DECAY) - ADAM_RATE * first_hat / (
        jnp.sqrt(second_hat) + ADAM_EPS
    )
    return (param_new, first_new, second_new)


def on_device(
    tokens,
    out_grad,
    doc_lengths,
    in_proj,
    inner_projection_weight,
    dt_proj,
    out_proj,
    in_moment,
    x_moment,
    dt_moment,
    out_moment,
    vectors,
    vector_first,
    vector_second,
    norm_gain,
    gain_first,
    gain_second,
):
    fsdp, ns = lax.axis_size("fsdp"), lax.axis_size("ns")
    shards = fsdp * ns
    per_device, columns = inner_projection_weight.shape
    rank, gains = dt_proj.shape[1], norm_gain.shape[0]
    block_out, grad_tokens, grad_gain, sum_in, sum_out, sum_small, sum_vec = layer(
        tokens,
        out_grad,
        doc_lengths,
        (
            in_proj,
            out_proj,
            inner_projection_weight,
            dt_proj,
            vectors,
            norm_gain[None],
        ),
        fsdp,
        ns,
    )
    sum_x = sum_small[:per_device, :columns]
    sum_dt = sum_small[:per_device, LANES : LANES + rank]
    summed = (sum_in, sum_x, sum_dt, sum_out, sum_vec)
    old_moments = (in_moment, x_moment, dt_moment, out_moment)
    moments = tuple((MOMENTUM * moment + grad for moment, grad in zip(old_moments, summed[:4])))
    gap = -per_device % 16
    low = jnp.stack(
        [
            jnp.pad(moments[1], ((0, gap), (0, LANES - columns))),
            jnp.pad(moments[2], ((0, gap), (0, LANES - rank))),
        ]
    )
    big, low, sum_gain = muon_rows(
        sum_in, sum_out, in_moment, out_moment, low, (columns, rank), grad_gain, fsdp, ns
    )
    place = lax.axis_index("fsdp") * ns + lax.axis_index("ns")
    sum_gain = lax.dynamic_slice_in_dim(sum_gain.reshape(-1), place * gains, gains, 0)
    own_blocks = (
        big[0],
        low[0, :per_device, :columns],
        low[1, :per_device, :rank],
        big[1, :per_device],
    )
    weights = (in_proj, inner_projection_weight, dt_proj, out_proj)
    fans = (DMODEL, DINNER, DTRANK, DINNER // 8)
    results = []
    for weight, moment, block, fan in zip(weights, moments, own_blocks, fans):
        rate = 0.5 * math.sqrt(weight.shape[0] * shards / fan)
        results.append((1.0 - SHRINK) * weight - rate * block.astype(jnp.float32))
        results.append(moment)
    vec_new, vec_first, vec_second = adamw_update(vectors, vector_first, vector_second, summed[4])
    gain_new, gain_m, gain_v = adamw_update(norm_gain, gain_first, gain_second, sum_gain)
    return (
        block_out,
        grad_tokens,
        results[0],
        results[1],
        results[2],
        results[3],
        results[4],
        results[5],
        results[6],
        results[7],
        vec_new,
        vec_first,
        vec_second,
        gain_new,
        gain_m,
        gain_v,
    )


def solution(mesh):
    placed = (
        P(("fsdp", "ns"), None, None),
        P(("fsdp", "ns"), None, None),
        P(("fsdp", "ns"), None),
        P(("fsdp", "ns"), None),
        P(("fsdp", "ns"), None),
        P(("fsdp", "ns"), None),
        P(("fsdp", "ns"), None),
        P(("fsdp", "ns"), None),
        P(("fsdp", "ns"), None),
        P(("fsdp", "ns"), None),
        P(("fsdp", "ns"), None),
        P(None, ("fsdp", "ns")),
        P(None, ("fsdp", "ns")),
        P(None, ("fsdp", "ns")),
        P(("fsdp", "ns")),
        P(("fsdp", "ns")),
        P(("fsdp", "ns")),
    )
    return jax.shard_map(
        on_device,
        mesh=mesh,
        in_specs=placed,
        out_specs=(
            P(("fsdp", "ns"), None, None),
            P(("fsdp", "ns"), None, None),
            P(("fsdp", "ns"), None),
            P(("fsdp", "ns"), None),
            P(("fsdp", "ns"), None),
            P(("fsdp", "ns"), None),
            P(("fsdp", "ns"), None),
            P(("fsdp", "ns"), None),
            P(("fsdp", "ns"), None),
            P(("fsdp", "ns"), None),
            P(None, ("fsdp", "ns")),
            P(None, ("fsdp", "ns")),
            P(None, ("fsdp", "ns")),
            P(("fsdp", "ns")),
            P(("fsdp", "ns")),
            P(("fsdp", "ns")),
        ),
        check_vma=False,
    )
```

time: 3860 us -> 302 us (0.08)
  waiting for transfers between devices: 1720 us -> 0 us
  other arithmetic: 1150 us -> 7.28 us
  blocking collectives: 416 us -> 0 us
  local copies, waits for them, and re-layouts: 336 us -> 3.77 us
  Pallas kernels: 0 us -> 289 us
  matrix products: 174 us -> 0 us
    reduce_scatter x16 -> x0, waiting for transfers between devices: 1250 us -> none  [the longest x1 362 us: on_device(): lax.psum_scatter(grads[0], ('fsdp', 'ns'), scatter_dimension=0, tiled=True)]
    while x708 -> x0, other arithmetic: 741 us -> none
    all_gather x13 -> x0, blocking collectives: 335 us -> none  [the longest x1 73 us: on_device(): lax.all_gather(lowered[2], ('fsdp', 'ns'), axis=0, tiled=True)]
    all_gather x12 -> x0, waiting for transfers between devices: 328 us -> none  [the longest x4 150 us: grams_by_groups(): lax.all_gather(rounded_shares[0], 'ns', axis=0, tiled=True)]
    pallas_call x0 -> x4, Pallas kernels: none -> 289 us  [the longest x1 76.1 us: muon_rows(): pl.pallas_call(functools.partial(muon_kernel, fsdp, ns, starts), in_specs...]
    dot_general x44 -> x0, matrix products: 174 us -> none  [the longest x24 90.3 us: contract(): lax.dot_general(left, right, (((left_dim,), (right_dim,)), ((), ())), pre...]
    dynamic_update_slice x152 -> x0, local copies, waits for them, and re-layouts: 155 us -> none  [the longest x128 138 us: block_states(): lax.scan(state_step, start, (jnp.moveaxis(decay, 1, 0), jnp.moveaxis(driv...]
    unnamed x38 -> x0, waiting for transfers between devices: 149 us -> none
  transfers between devices with their start and end apart: 33 -> 0, of which waited for: 30 -> 0; matrix products, arithmetic and copies ran while one was open for 15% -> 0% of each run, Pallas kernels for 0% -> 0%
where the time goes in v1:
time: 302 us; the launch traced here: 301 us
  Pallas kernels  289 us (96%)
  other arithmetic  7.28 us (2%)
  local copies, waits for them, and re-layouts  3.77 us (1%)
    pallas_call x1, Pallas kernels, muon_rows(): pl.pallas_call(functools.partial(muon_kernel, fsdp, ns, starts), in_specs...  76.1 us
    pallas_call x1, Pallas kernels, back_and_scatter(): pl.pallas_call(functools.partial(back_kernel, fsdp, ns, per_device), in_s...  75.6 us
    pallas_call x1, Pallas kernels, gather_and_front(): pl.pallas_call(functools.partial(front_kernel, fsdp, ns, per_device, gain...  73.9 us
    pallas_call x1, Pallas kernels, scan_both(): pl.pallas_call(scan_kernel, grid=(inner // PASS,), in_specs=[pl.BlockSpec...  63.6 us

profile of v1, /device:TPU:0, one launch (start us, length us, event | category | flops | bytes accessed | tf_op | source)
XLA Modules:
  0.0 301.1 jit_solution(6785993773909088874)
XLA Ops:
  0.6 73.9 %shard_map.288 = (bf16[32,128,1024]{2,1,0:T(8,128)(2,1)}, bf16[32,64,1024]{2,1,0:T(8,128)(2,1)}, bf16[2048,128]{1,0:T(8,128)(2,1)}, bf16[2048,128]{1,0:T(8,128)(...) custom-call(s32[1,4]{1,0:T(1,128)} %lengths_ref.1, ...), custom_call_target="tpu_custom_call" | custom-call | tf_op jit(solution)/shard_map/pallas_call | solution.py:853
  74.6 63.6 %shard_map.289 = (bf16[256,2048]{1,0:T(8,128)(2,1)}, f32[256,2048]{1,0:T(8,128)}, bf16[256,2048]{1,0:T(8,128)(2,1)}, f32[16,2048]{1,0:T(8,128)}, f32[16,2048]{1,...) custom-call(f32[256,128]{1,0:T(8,128)} %get-tuple-element.47.bc_ref.proj_ref, ...), custom_call_target="tpu_custom_call" | custom-call | flops 201326592 | bytes 12582912 | tf_op jit(solution)/shard_map/pallas_call | solution.py:298
  138.2 0.0 copy-start.15
  138.2 0.0 copy-start.16
  138.2 0.0 copy-start
  138.2 0.0 copy-start.3
  138.2 0.0 copy-start.7
  138.2 75.6 %shard_map.290 = (f32[256,1024]{1,0:T(8,128)}, f32[16,128]{1,0:T(8,128)}, f32[128,1024]{1,0:T(8,128)}, f32[64,1024]{1,0:T(8,128)}, f32[64,256]{1,0:T(8,128)}, /*index=5*/f32[23,64]{1,0:T(8,128)}) custom-call(bf16[32,64,1024]{2,1,0:T(8,128)(2,1)} %bitcast.22, bf16[256,2048]{1,0:T(8,128)(2,1)} %get-tuple-element.56.far_1_, ...), custom_call_target="tpu_custom_call" | custom-call | tf_op jit(solution)/shard_map/pallas_call | solution.py:1279
  213.9 0.0 copy-start.9
  213.9 0.0 copy-start.10
  213.9 0.0 copy-start.11
  213.9 0.0 copy-done.15
  213.9 0.8 slice_add_fusion
  214.7 0.0 copy-done.16
  214.7 0.0 copy-start.12
  214.7 0.0 copy-start.20
  214.8 0.0 copy-start.21
  214.8 0.0 copy-start.22
  214.8 0.8 slice_add_fusion.1
  215.6 0.0 copy-done
  215.6 0.0 copy-done.3
  215.6 0.0 copy-start.1
  215.6 1.0 copy-done.1
  216.7 0.9 copy-done.4
  217.6 0.7 copy-done.6
  218.3 76.1 %shard_map.291 = (bf16[2,128,1024]{2,1,0:T(8,128)(2,1)S(1)}, bf16[2,64,128]{2,1,0:T(8,128)(2,1)S(1)}, f32[16,128]{1,0:T(8,128)S(1)}) custom-call(f32[128,1024]{1,0:T(8,128)S(1)} %copy-done.1, f32[64,1024]{1,0:T(8,128)S(1)} %copy-done.4, f32[128,1024]{1,0:T(8,128)S(1)} %copy-done, f32[64,1024]{1,0:T(8,128)S(1)} %copy-done.3, ...), custom_call_target="tpu_custom_call" | custom-call | tf_op jit(solution)/shard_map/pallas_call | solution.py:1618
  294.4 0.0 copy-start.5
  294.4 0.0 copy-done.7
  294.4 0.0 copy-start.14
  294.4 0.0 copy-start.17
  294.4 0.0 copy-start.18
  294.4 0.0 copy-start.19
  294.4 0.0 copy-start.8
  294.4 0.9 convert_subtract_fusion
  295.3 0.0 copy-done.9
  295.3 0.7 bitcast_subtract_fusion
  296.1 0.0 copy-done.10
  296.1 0.6 bitcast_subtract_fusion.1
  296.7 0.6 bitcast_subtract_fusion.2
  297.3 0.0 copy-done.20
  297.3 0.0 copy-done.22
  297.3 0.6 divide_subtract_fusion.1
  297.9 0.9 multiply_add_fusion
  298.8 0.0 copy-done.12
  298.8 0.7 multiply_add_fusion.1
  299.5 0.0 copy-done.17
  299.6 0.6 divide_subtract_fusion
  300.2 1.0 copy.34
  (15 shorter events, 0.0 us)
Async XLA Ops:
  138.2 75.7 %copy-start.15 = (f32[64,64]{1,0:T(8,128)S(1)}, f32[64,64]{1,0:T(8,128)}, u32[]{:S(2)}) copy-start(f32[64,64]{1,0:T(8,128)} %param.26) | copy-start | bytes 49156
  138.2 76.5 %copy-start.16 = (f32[64,96]{1,0:T(8,128)S(1)}, f32[64,96]{1,0:T(8,128)}, u32[]{:S(2)}) copy-start(f32[64,96]{1,0:T(8,128)} %param.25) | copy-start | bytes 73732
  138.2 77.4 %copy-start = (f32[128,1024]{1,0:T(8,128)S(1)}, f32[128,1024]{1,0:T(8,128)}, u32[]{:S(2)}) copy-start(f32[128,1024]{1,0:T(8,128)} %in_moment.1) | copy-start | bytes 1572868
  138.2 77.4 %copy-start.3 = (f32[64,1024]{1,0:T(8,128)S(1)}, f32[64,1024]{1,0:T(8,128)}, u32[]{:S(2)}) copy-start(f32[64,1024]{1,0:T(8,128)} %out_moment.1) | copy-start | bytes 786436
  138.2 156.2 %copy-start.7 = (f32[128,1024]{1,0:T(8,128)S(1)}, f32[128,1024]{1,0:T(8,128)}, u32[]{:S(2)}) copy-start(f32[128,1024]{1,0:T(8,128)} %in_ref.1) | copy-start | bytes 1572868
  213.9 81.4 %copy-start.9 = (f32[64,1024]{1,0:T(8,128)S(1)}, f32[64,1024]{1,0:T(8,128)}, u32[]{:S(2)}) copy-start(f32[64,1024]{1,0:T(8,128)} %out_ref.1) | copy-start | bytes 786436
  213.9 82.2 %copy-start.10 = (f32[64,64]{1,0:T(8,128)S(1)}, f32[64,64]{1,0:T(8,128)}, u32[]{:S(2)}) copy-start(f32[64,64]{1,0:T(8,128)} %dt_own.1) | copy-start | bytes 49156
  213.9 82.8 %copy-start.11 = (f32[64,96]{1,0:T(8,128)S(1)}, f32[64,96]{1,0:T(8,128)}, u32[]{:S(2)}) copy-start(f32[64,96]{1,0:T(8,128)} %x_own.1) | copy-start | bytes 73732
  214.7 84.1 %copy-start.12 = (f32[64,64]{1,0:T(8,128)}, f32[64,64]{1,0:T(8,128)S(1)}, u32[]{:S(2)}) copy-start(f32[64,64]{1,0:T(8,128)S(1)} %slice_add_fusion) | copy-start | bytes 49156
  214.7 82.6 %copy-start.20 = (f32[32]{0:T(128)S(1)}, f32[32]{0:T(128)}, u32[]{:S(2)}) copy-start(f32[32]{0:T(128)} %param.31) | copy-start | bytes 388
  214.8 82.6 %copy-start.21 = (f32[32]{0:T(128)S(1)}, f32[32]{0:T(128)}, u32[]{:S(2)}) copy-start(f32[32]{0:T(128)} %param.32) | copy-start | bytes 388
  214.8 82.6 %copy-start.22 = (f32[32]{0:T(128)S(1)}, f32[32]{0:T(128)}, u32[]{:S(2)}) copy-start(f32[32]{0:T(128)} %param.33) | copy-start | bytes 388
  215.6 83.2 %copy-start.13 = (f32[64,96]{1,0:T(8,128)}, f32[64,96]{1,0:T(8,128)S(1)}, u32[]{:S(2)}) copy-start(f32[64,96]{1,0:T(8,128)S(1)} %slice_add_fusion.1) | copy-start | bytes 73732
  215.6 1.0 copy-start.1
  216.7 0.9 copy-start.4
  217.6 0.7 copy-start.6
  218.3 79.6 %copy-start.2 = (f32[128,1024]{1,0:T(8,128)S(1)}, f32[128,1024]{1,0:T(8,128)}, u32[]{:S(2)}) copy-start(f32[128,1024]{1,0:T(8,128)} %get-tuple-element.70.sum_in) | copy-start | bytes 1572868
  294.4 4.4 %copy-start.5 = (f32[64,1024]{1,0:T(8,128)S(1)}, f32[64,1024]{1,0:T(8,128)}, u32[]{:S(2)}) copy-start(f32[64,1024]{1,0:T(8,128)} %get-tuple-element.71.sum_out) | copy-start | bytes 786436
  294.4 5.1 %copy-start.14 = (f32[23,64]{1,0:T(8,128)S(1)}, f32[23,64]{1,0:T(8,128)}, u32[]{:S(2)}) copy-start(f32[23,64]{1,0:T(8,128)} %vectors_own.1) | copy-start | bytes 17668
  294.4 5.1 %copy-start.17 = (f32[23,64]{1,0:T(8,128)S(1)}, f32[23,64]{1,0:T(8,128)}, u32[]{:S(2)}) copy-start(f32[23,64]{1,0:T(8,128)} %param.29) | copy-start | bytes 17668
  294.4 5.1 %copy-start.18 = (f32[23,64]{1,0:T(8,128)S(1)}, f32[23,64]{1,0:T(8,128)}, u32[]{:S(2)}) copy-start(f32[23,64]{1,0:T(8,128)} %param.30) | copy-start | bytes 17668
  294.4 5.1 %copy-start.19 = (f32[23,64]{1,0:T(8,128)S(1)}, f32[23,64]{1,0:T(8,128)}, u32[]{:S(2)}) copy-start(f32[23,64]{1,0:T(8,128)} %get-tuple-element.76) | copy-start | bytes 17668
  294.4 5.7 %copy-start.8 = (f32[256,1024]{1,0:T(8,128)S(1)}, f32[256,1024]{1,0:T(8,128)}, u32[]{:S(2)}) copy-start(f32[256,1024]{1,0:T(8,128)} %get-tuple-element.69) | copy-start | bytes 3145732

commit v2 on v1

--- a/solution.py
+++ b/solution.py
@@ -228,14 +228,11 @@
     total = jnp.zeros((length, LANES), jnp.float32)
     for n in range(DSTATE):
         goes = jnp.where(first, DTRANK + n, DTRANK + DSTATE + n) == column
-        goes = goes.astype(jnp.bfloat16)
-        for side, sums in enumerate((sums_b, sums_c)):
-            value = sums[pl.ds(n, length, stride=DSTATE), :]
-            upper = value.astype(jnp.bfloat16)
-            lower = (value - upper.astype(jnp.float32)).astype(jnp.bfloat16)
-            part = goes[side * LANES : (side + 1) * LANES, :]
-            total = total + jnp.dot(upper, part, preferred_element_type=jnp.float32)
-            total = total + jnp.dot(lower, part, preferred_element_type=jnp.float32)
+        at = (pl.ds(n, length, stride=DSTATE), slice(None))
+        both = jnp.concatenate([sums_b[at], sums_c[at]], axis=1).astype(jnp.bfloat16)
+        total = total + jnp.dot(
+            both, goes.astype(jnp.bfloat16), preferred_element_type=jnp.float32
+        )
 
     @pl.when(half == 0)
     def _():

time: 302 us -> 298 us (0.987)
  Pallas kernels: 289 us -> 285 us
    pallas_call x1, Pallas kernels: 63.6 us -> 59.4 us  [scan_both(): pl.pallas_call(scan_kernel, grid=(inner // PASS,), in_specs=[pl.BlockSpec...]
where the time goes in v2:
time: 298 us; the launch traced here: 297 us
  Pallas kernels  285 us (96%)
  other arithmetic  7.28 us (2%)
  local copies, waits for them, and re-layouts  3.77 us (1%)
    pallas_call x1, Pallas kernels, muon_rows(): pl.pallas_call(functools.partial(muon_kernel, fsdp, ns, starts), in_specs...  76.1 us
    pallas_call x1, Pallas kernels, back_and_scatter(): pl.pallas_call(functools.partial(back_kernel, fsdp, ns, per_device), in_s...  75.6 us
    pallas_call x1, Pallas kernels, gather_and_front(): pl.pallas_call(functools.partial(front_kernel, fsdp, ns, per_device, gain...  73.9 us
    pallas_call x1, Pallas kernels, scan_both(): pl.pallas_call(scan_kernel, grid=(inner // PASS,), in_specs=[pl.BlockSpec...  59.4 us

profile of v2, /device:TPU:0, one launch (start us, length us, event | category | flops | bytes accessed | tf_op | source)
XLA Modules:
  0.0 297.0 jit_solution(8651762225327045752)
XLA Ops:
  0.6 73.9 %shard_map.288 = (bf16[32,128,1024]{2,1,0:T(8,128)(2,1)}, bf16[32,64,1024]{2,1,0:T(8,128)(2,1)}, bf16[2048,128]{1,0:T(8,128)(2,1)}, bf16[2048,128]{1,0:T(8,128)(...) custom-call(s32[1,4]{1,0:T(1,128)} %lengths_ref.1, ...), custom_call_target="tpu_custom_call" | custom-call | tf_op jit(solution)/shard_map/pallas_call | solution.py:850
  74.6 59.4 %shard_map.289 = (bf16[256,2048]{1,0:T(8,128)(2,1)}, f32[256,2048]{1,0:T(8,128)}, bf16[256,2048]{1,0:T(8,128)(2,1)}, f32[16,2048]{1,0:T(8,128)}, f32[16,2048]{1,...) custom-call(f32[256,128]{1,0:T(8,128)} %get-tuple-element.47.bc_ref.proj_ref, ...), custom_call_target="tpu_custom_call" | custom-call | flops 201326592 | bytes 12582912 | tf_op jit(solution)/shard_map/pallas_call | solution.py:295
  134.0 0.0 copy-start.15
  134.0 0.0 copy-start.16
  134.1 0.0 copy-start
  134.1 0.0 copy-start.3
  134.1 0.0 copy-start.7
  134.1 75.6 %shard_map.290 = (f32[256,1024]{1,0:T(8,128)}, f32[16,128]{1,0:T(8,128)}, f32[128,1024]{1,0:T(8,128)}, f32[64,1024]{1,0:T(8,128)}, f32[64,256]{1,0:T(8,128)}, /*index=5*/f32[23,64]{1,0:T(8,128)}) custom-call(bf16[32,64,1024]{2,1,0:T(8,128)(2,1)} %bitcast.22, bf16[256,2048]{1,0:T(8,128)(2,1)} %get-tuple-element.56.far_1_, ...), custom_call_target="tpu_custom_call" | custom-call | tf_op jit(solution)/shard_map/pallas_call | solution.py:1276
  209.7 0.0 copy-start.9
  209.7 0.0 copy-start.10
  209.7 0.0 copy-start.11
  209.7 0.0 copy-done.15
  209.7 0.8 slice_add_fusion
  210.5 0.0 copy-done.16
  210.5 0.0 copy-start.12
  210.6 0.0 copy-start.20
  210.6 0.0 copy-start.21
  210.6 0.0 copy-start.22
  210.6 0.8 slice_add_fusion.1
  211.4 0.0 copy-done
  211.4 0.0 copy-done.3
  211.4 0.0 copy-start.1
  211.4 1.0 copy-done.1
  212.5 0.9 copy-done.4
  213.4 0.7 copy-done.6
  214.1 76.1 %shard_map.291 = (bf16[2,128,1024]{2,1,0:T(8,128)(2,1)S(1)}, bf16[2,64,128]{2,1,0:T(8,128)(2,1)S(1)}, f32[16,128]{1,0:T(8,128)S(1)}) custom-call(f32[128,1024]{1,0:T(8,128)S(1)} %copy-done.1, f32[64,1024]{1,0:T(8,128)S(1)} %copy-done.4, f32[128,1024]{1,0:T(8,128)S(1)} %copy-done, f32[64,1024]{1,0:T(8,128)S(1)} %copy-done.3, ...), custom_call_target="tpu_custom_call" | custom-call | tf_op jit(solution)/shard_map/pallas_call | solution.py:1615
  290.2 0.0 copy-start.5
  290.2 0.0 copy-done.7
  290.2 0.0 copy-start.14
  290.2 0.0 copy-start.17
  290.2 0.0 copy-start.18
  290.3 0.0 copy-start.19
  290.3 0.0 copy-start.8
  290.3 0.9 convert_subtract_fusion
  291.1 0.0 copy-done.9
  291.1 0.7 bitcast_subtract_fusion
  291.9 0.0 copy-done.10
  291.9 0.6 bitcast_subtract_fusion.1
  292.5 0.0 copy-done.11
  292.5 0.6 bitcast_subtract_fusion.2
  293.2 0.6 divide_subtract_fusion.1
  293.8 0.9 multiply_add_fusion
  294.6 0.0 copy-done.13
  294.6 0.7 multiply_add_fusion.1
  295.4 0.0 copy-done.14
  295.4 0.0 copy-done.18
  295.4 0.6 divide_subtract_fusion
  296.0 1.0 copy.34
  (15 shorter events, 0.0 us)
Async XLA Ops:
  134.0 75.7 %copy-start.15 = (f32[64,64]{1,0:T(8,128)S(1)}, f32[64,64]{1,0:T(8,128)}, u32[]{:S(2)}) copy-start(f32[64,64]{1,0:T(8,128)} %param.26) | copy-start | bytes 49156
  134.0 76.5 %copy-start.16 = (f32[64,96]{1,0:T(8,128)S(1)}, f32[64,96]{1,0:T(8,128)}, u32[]{:S(2)}) copy-start(f32[64,96]{1,0:T(8,128)} %param.25) | copy-start | bytes 73732
  134.1 77.4 %copy-start = (f32[128,1024]{1,0:T(8,128)S(1)}, f32[128,1024]{1,0:T(8,128)}, u32[]{:S(2)}) copy-start(f32[128,1024]{1,0:T(8,128)} %in_moment.1) | copy-start | bytes 1572868
  134.1 77.3 %copy-start.3 = (f32[64,1024]{1,0:T(8,128)S(1)}, f32[64,1024]{1,0:T(8,128)}, u32[]{:S(2)}) copy-start(f32[64,1024]{1,0:T(8,128)} %out_moment.1) | copy-start | bytes 786436
  134.1 156.1 %copy-start.7 = (f32[128,1024]{1,0:T(8,128)S(1)}, f32[128,1024]{1,0:T(8,128)}, u32[]{:S(2)}) copy-start(f32[128,1024]{1,0:T(8,128)} %in_ref.1) | copy-start | bytes 1572868
  209.7 81.5 %copy-start.9 = (f32[64,1024]{1,0:T(8,128)S(1)}, f32[64,1024]{1,0:T(8,128)}, u32[]{:S(2)}) copy-start(f32[64,1024]{1,0:T(8,128)} %out_ref.1) | copy-start | bytes 786436
  209.7 82.2 %copy-start.10 = (f32[64,64]{1,0:T(8,128)S(1)}, f32[64,64]{1,0:T(8,128)}, u32[]{:S(2)}) copy-start(f32[64,64]{1,0:T(8,128)} %dt_own.1) | copy-start | bytes 49156
  209.7 82.8 %copy-start.11 = (f32[64,96]{1,0:T(8,128)S(1)}, f32[64,96]{1,0:T(8,128)}, u32[]{:S(2)}) copy-start(f32[64,96]{1,0:T(8,128)} %x_own.1) | copy-start | bytes 73732
  210.5 84.1 %copy-start.12 = (f32[64,64]{1,0:T(8,128)}, f32[64,64]{1,0:T(8,128)S(1)}, u32[]{:S(2)}) copy-start(f32[64,64]{1,0:T(8,128)S(1)} %slice_add_fusion) | copy-start | bytes 49156
  210.6 82.6 %copy-start.20 = (f32[32]{0:T(128)S(1)}, f32[32]{0:T(128)}, u32[]{:S(2)}) copy-start(f32[32]{0:T(128)} %param.31) | copy-start | bytes 388
  210.6 82.6 %copy-start.21 = (f32[32]{0:T(128)S(1)}, f32[32]{0:T(128)}, u32[]{:S(2)}) copy-start(f32[32]{0:T(128)} %param.32) | copy-start | bytes 388
  210.6 82.6 %copy-start.22 = (f32[32]{0:T(128)S(1)}, f32[32]{0:T(128)}, u32[]{:S(2)}) copy-start(f32[32]{0:T(128)} %param.33) | copy-start | bytes 388
  211.4 83.2 %copy-start.13 = (f32[64,96]{1,0:T(8,128)}, f32[64,96]{1,0:T(8,128)S(1)}, u32[]{:S(2)}) copy-start(f32[64,96]{1,0:T(8,128)S(1)} %slice_add_fusion.1) | copy-start | bytes 73732
  211.4 1.0 copy-start.1
  212.5 0.9 copy-start.4
  213.4 0.7 copy-start.6
  214.1 79.6 %copy-start.2 = (f32[128,1024]{1,0:T(8,128)S(1)}, f32[128,1024]{1,0:T(8,128)}, u32[]{:S(2)}) copy-start(f32[128,1024]{1,0:T(8,128)} %get-tuple-element.70.sum_in) | copy-start | bytes 1572868
  290.2 4.4 %copy-start.5 = (f32[64,1024]{1,0:T(8,128)S(1)}, f32[64,1024]{1,0:T(8,128)}, u32[]{:S(2)}) copy-start(f32[64,1024]{1,0:T(8,128)} %get-tuple-element.71.sum_out) | copy-start | bytes 786436
  290.2 5.1 %copy-start.14 = (f32[23,64]{1,0:T(8,128)S(1)}, f32[23,64]{1,0:T(8,128)}, u32[]{:S(2)}) copy-start(f32[23,64]{1,0:T(8,128)} %vectors_own.1) | copy-start | bytes 17668
  290.2 5.1 %copy-start.17 = (f32[23,64]{1,0:T(8,128)S(1)}, f32[23,64]{1,0:T(8,128)}, u32[]{:S(2)}) copy-start(f32[23,64]{1,0:T(8,128)} %param.29) | copy-start | bytes 17668
  290.2 5.1 %copy-start.18 = (f32[23,64]{1,0:T(8,128)S(1)}, f32[23,64]{1,0:T(8,128)}, u32[]{:S(2)}) copy-start(f32[23,64]{1,0:T(8,128)} %param.30) | copy-start | bytes 17668
  290.3 5.1 %copy-start.19 = (f32[23,64]{1,0:T(8,128)S(1)}, f32[23,64]{1,0:T(8,128)}, u32[]{:S(2)}) copy-start(f32[23,64]{1,0:T(8,128)} %get-tuple-element.76) | copy-start | bytes 17668
  290.3 5.7 %copy-start.8 = (f32[256,1024]{1,0:T(8,128)S(1)}, f32[256,1024]{1,0:T(8,128)}, u32[]{:S(2)}) copy-start(f32[256,1024]{1,0:T(8,128)} %get-tuple-element.69) | copy-start | bytes 3145732

commit v3 on v2

--- a/solution.py
+++ b/solution.py
@@ -158,19 +158,23 @@
     zero = jnp.zeros((SUBS, LANES), jnp.float32)
     lax.fori_loop(0, length // STEPS, ahead, (zero,) * DSTATE)
 
+    fold = SUBS // 2
+    span = DSTATE * fold
     pick = (
-        lax.broadcasted_iota(jnp.int32, (2 * DSTATE, 2 * LANES), 1) // SUBS
-        == lax.broadcasted_iota(jnp.int32, (2 * DSTATE, 2 * LANES), 0)
+        lax.broadcasted_iota(jnp.int32, (STEPS * DSTATE, STEPS * span), 1) // fold
+        == lax.broadcasted_iota(jnp.int32, (STEPS * DSTATE, STEPS * span), 0)
     ).astype(jnp.bfloat16)
-    span = DSTATE * SUBS
+    upper = lax.broadcasted_iota(jnp.int32, (SUBS, LANES), 0) < fold
+
+    def folded(one, two):
+        crossed = pltpu.roll(jnp.where(upper, two, one), fold, 0)
+        return jnp.where(upper, one, two) + crossed
 
     def channel_sums(products, t0):
-        for k in range(0, STEPS, 2):
-            block = products[k * span : (k + 2) * span, :]
-            row = pl.multiple_of((t0 + k) * DSTATE, 2 * DSTATE)
-            both = jnp.dot(pick, block, preferred_element_type=jnp.float32)
-            sums_b[pl.ds(row, 2 * DSTATE), :] = both[:, 0:LANES]
-            sums_c[pl.ds(row, 2 * DSTATE), :] = both[:, LANES : 2 * LANES]
+        row = pl.multiple_of(t0 * DSTATE, STEPS * DSTATE)
+        both = jnp.dot(pick, products[...], preferred_element_type=jnp.float32)
+        sums_b[pl.ds(row, STEPS * DSTATE), :] = both[:, 0:LANES]
+        sums_c[pl.ds(row, STEPS * DSTATE), :] = both[:, LANES : 2 * LANES]
 
     def behind_steps(t0, products, flow, g_amat):
         for k in reversed(range(STEPS)):
@@ -191,12 +195,16 @@
                 prod_b_n = adj * drive
                 prod_c_n = states[(t + 1) * DSTATE + n] * dstate
                 if n % 2:
-                    row = k * span + (n - 1) * SUBS
+                    pair_b, pair_c = folded(pend_b, prod_b_n), folded(pend_c, prod_c_n)
+                if n % 4 == 1:
+                    half_b, half_c = pair_b, pair_c
+                if n % 4 == 3:
+                    row = k * span + (n - 3) * fold
                     products[row : row + 2 * SUBS, 0:LANES] = jnp.concatenate(
-                        [pend_b, prod_b_n], axis=0
+                        [half_b, pair_b], axis=0
                     ).astype(jnp.bfloat16)
                     products[row : row + 2 * SUBS, LANES : 2 * LANES] = jnp.concatenate(
-                        [pend_c, prod_c_n], axis=0
+                        [half_c, pair_c], axis=0
                     ).astype(jnp.bfloat16)
                 pend_b, pend_c = prod_b_n, prod_c_n
             put_tile(pull_s, t, pull[0] + pull[1])
@@ -336,8 +344,8 @@
         + [pltpu.VMEM((length * SUBS, LANES), f32)] * 6
         + [
             pltpu.VMEM(((length + 1) * DSTATE, SUBS, LANES), f32),
-            pltpu.VMEM((STEPS * DSTATE * SUBS, 2 * LANES), b16),
-            pltpu.VMEM((STEPS * DSTATE * SUBS, 2 * LANES), b16),
+            pltpu.VMEM((STEPS * DSTATE * SUBS // 2, 2 * LANES), b16),
+            pltpu.VMEM((STEPS * DSTATE * SUBS // 2, 2 * LANES), b16),
             pltpu.VMEM(((length + STEPS) * DSTATE, LANES), f32),
             pltpu.VMEM(((length + STEPS) * DSTATE, LANES), f32),
         ],

time: 298 us -> 301 us (1.010)
  no operation moved by 1% of the time
where the time goes in v3:
time: 301 us; the launch traced here: 300 us
  Pallas kernels  288 us (96%)
  other arithmetic  7.28 us (2%)
  local copies, waits for them, and re-layouts  3.77 us (1%)
    pallas_call x1, Pallas kernels, muon_rows(): pl.pallas_call(functools.partial(muon_kernel, fsdp, ns, starts), in_specs...  76.1 us
    pallas_call x1, Pallas kernels, back_and_scatter(): pl.pallas_call(functools.partial(back_kernel, fsdp, ns, per_device), in_s...  75.6 us
    pallas_call x1, Pallas kernels, gather_and_front(): pl.pallas_call(functools.partial(front_kernel, fsdp, ns, per_device, gain...  73.9 us
    pallas_call x1, Pallas kernels, scan_both(): pl.pallas_call(scan_kernel, grid=(inner // PASS,), in_specs=[pl.BlockSpec...  62 us

profile of v3, /device:TPU:0, one launch (start us, length us, event | category | flops | bytes accessed | tf_op | source)
XLA Modules:
  0.0 299.5 jit_solution(17016545493226144743)
XLA Ops:
  0.6 73.9 %shard_map.288 = (bf16[32,128,1024]{2,1,0:T(8,128)(2,1)}, bf16[32,64,1024]{2,1,0:T(8,128)(2,1)}, bf16[2048,128]{1,0:T(8,128)(2,1)}, bf16[2048,128]{1,0:T(8,128)(...) custom-call(s32[1,4]{1,0:T(1,128)} %lengths_ref.1, ...), custom_call_target="tpu_custom_call" | custom-call | tf_op jit(solution)/shard_map/pallas_call | solution.py:858
  74.6 62.0 %shard_map.289 = (bf16[256,2048]{1,0:T(8,128)(2,1)}, f32[256,2048]{1,0:T(8,128)}, bf16[256,2048]{1,0:T(8,128)(2,1)}, f32[16,2048]{1,0:T(8,128)}, f32[16,2048]{1,...) custom-call(f32[256,128]{1,0:T(8,128)} %get-tuple-element.47.bc_ref.proj_ref, ...), custom_call_target="tpu_custom_call" | custom-call | flops 201326592 | bytes 12582912 | tf_op jit(solution)/shard_map/pallas_call | solution.py:303
  136.6 0.0 copy-start.15
  136.6 0.0 copy-start.16
  136.6 0.0 copy-start
  136.6 0.0 copy-start.3
  136.7 0.0 copy-start.7
  136.7 75.6 %shard_map.290 = (f32[256,1024]{1,0:T(8,128)}, f32[16,128]{1,0:T(8,128)}, f32[128,1024]{1,0:T(8,128)}, f32[64,1024]{1,0:T(8,128)}, f32[64,256]{1,0:T(8,128)}, /*index=5*/f32[23,64]{1,0:T(8,128)}) custom-call(bf16[32,64,1024]{2,1,0:T(8,128)(2,1)} %bitcast.22, bf16[256,2048]{1,0:T(8,128)(2,1)} %get-tuple-element.56.far_1_, ...), custom_call_target="tpu_custom_call" | custom-call | tf_op jit(solution)/shard_map/pallas_call | solution.py:1284
  212.3 0.0 copy-start.9
  212.3 0.0 copy-start.10
  212.3 0.0 copy-start.11
  212.3 0.0 copy-done.15
  212.3 0.8 slice_add_fusion
  213.1 0.0 copy-done.16
  213.1 0.0 copy-start.12
  213.1 0.0 copy-start.20
  213.1 0.0 copy-start.21
  213.2 0.0 copy-start.22
  213.2 0.8 slice_add_fusion.1
  214.0 0.0 copy-done
  214.0 0.0 copy-done.3
  214.0 0.0 copy-start.1
  214.0 1.0 copy-done.1
  215.1 0.9 copy-done.4
  216.0 0.7 copy-done.6
  216.7 76.1 %shard_map.291 = (bf16[2,128,1024]{2,1,0:T(8,128)(2,1)S(1)}, bf16[2,64,128]{2,1,0:T(8,128)(2,1)S(1)}, f32[16,128]{1,0:T(8,128)S(1)}) custom-call(f32[128,1024]{1,0:T(8,128)S(1)} %copy-done.1, f32[64,1024]{1,0:T(8,128)S(1)} %copy-done.4, f32[128,1024]{1,0:T(8,128)S(1)} %copy-done, f32[64,1024]{1,0:T(8,128)S(1)} %copy-done.3, ...), custom_call_target="tpu_custom_call" | custom-call | tf_op jit(solution)/shard_map/pallas_call | solution.py:1623
  292.8 0.0 copy-start.5
  292.8 0.0 copy-done.7
  292.8 0.0 copy-start.14
  292.8 0.0 copy-start.17
  292.8 0.0 copy-start.18
  292.8 0.0 copy-start.19
  292.8 0.0 copy-start.8
  292.8 0.9 convert_subtract_fusion
  293.7 0.0 copy-done.9
  293.7 0.7 bitcast_subtract_fusion
  294.5 0.0 copy-done.10
  294.5 0.6 bitcast_subtract_fusion.1
  295.1 0.6 bitcast_subtract_fusion.2
  295.7 0.0 copy-done.22
  295.7 0.6 divide_subtract_fusion.1
  296.3 0.9 multiply_add_fusion
  297.2 0.0 copy-done.12
  297.2 0.0 copy-done.5
  297.2 0.7 multiply_add_fusion.1
  297.9 0.0 copy-done.17
  297.9 0.6 divide_subtract_fusion
  298.6 1.0 copy.34
  (15 shorter events, 0.0 us)
Async XLA Ops:
  136.6 75.7 %copy-start.15 = (f32[64,64]{1,0:T(8,128)S(1)}, f32[64,64]{1,0:T(8,128)}, u32[]{:S(2)}) copy-start(f32[64,64]{1,0:T(8,128)} %param.26) | copy-start | bytes 49156
  136.6 76.5 %copy-start.16 = (f32[64,96]{1,0:T(8,128)S(1)}, f32[64,96]{1,0:T(8,128)}, u32[]{:S(2)}) copy-start(f32[64,96]{1,0:T(8,128)} %param.25) | copy-start | bytes 73732
  136.6 77.4 %copy-start = (f32[128,1024]{1,0:T(8,128)S(1)}, f32[128,1024]{1,0:T(8,128)}, u32[]{:S(2)}) copy-start(f32[128,1024]{1,0:T(8,128)} %in_moment.1) | copy-start | bytes 1572868
  136.6 77.4 %copy-start.3 = (f32[64,1024]{1,0:T(8,128)S(1)}, f32[64,1024]{1,0:T(8,128)}, u32[]{:S(2)}) copy-start(f32[64,1024]{1,0:T(8,128)} %out_moment.1) | copy-start | bytes 786436
  136.7 156.1 %copy-start.7 = (f32[128,1024]{1,0:T(8,128)S(1)}, f32[128,1024]{1,0:T(8,128)}, u32[]{:S(2)}) copy-start(f32[128,1024]{1,0:T(8,128)} %in_ref.1) | copy-start | bytes 1572868
  212.3 81.4 %copy-start.9 = (f32[64,1024]{1,0:T(8,128)S(1)}, f32[64,1024]{1,0:T(8,128)}, u32[]{:S(2)}) copy-start(f32[64,1024]{1,0:T(8,128)} %out_ref.1) | copy-start | bytes 786436
  212.3 82.2 %copy-start.10 = (f32[64,64]{1,0:T(8,128)S(1)}, f32[64,64]{1,0:T(8,128)}, u32[]{:S(2)}) copy-start(f32[64,64]{1,0:T(8,128)} %dt_own.1) | copy-start | bytes 49156
  212.3 82.8 %copy-start.11 = (f32[64,96]{1,0:T(8,128)S(1)}, f32[64,96]{1,0:T(8,128)}, u32[]{:S(2)}) copy-start(f32[64,96]{1,0:T(8,128)} %x_own.1) | copy-start | bytes 73732
  213.1 84.1 %copy-start.12 = (f32[64,64]{1,0:T(8,128)}, f32[64,64]{1,0:T(8,128)S(1)}, u32[]{:S(2)}) copy-start(f32[64,64]{1,0:T(8,128)S(1)} %slice_add_fusion) | copy-start | bytes 49156
  213.1 82.6 %copy-start.20 = (f32[32]{0:T(128)S(1)}, f32[32]{0:T(128)}, u32[]{:S(2)}) copy-start(f32[32]{0:T(128)} %param.31) | copy-start | bytes 388
  213.1 82.6 %copy-start.21 = (f32[32]{0:T(128)S(1)}, f32[32]{0:T(128)}, u32[]{:S(2)}) copy-start(f32[32]{0:T(128)} %param.32) | copy-start | bytes 388
  213.2 82.6 %copy-start.22 = (f32[32]{0:T(128)S(1)}, f32[32]{0:T(128)}, u32[]{:S(2)}) copy-start(f32[32]{0:T(128)} %param.33) | copy-start | bytes 388
  214.0 83.2 %copy-start.13 = (f32[64,96]{1,0:T(8,128)}, f32[64,96]{1,0:T(8,128)S(1)}, u32[]{:S(2)}) copy-start(f32[64,96]{1,0:T(8,128)S(1)} %slice_add_fusion.1) | copy-start | bytes 73732
  214.0 1.0 copy-start.1
  215.1 0.9 copy-start.4
  216.0 0.7 copy-start.6
  216.7 79.6 %copy-start.2 = (f32[128,1024]{1,0:T(8,128)S(1)}, f32[128,1024]{1,0:T(8,128)}, u32[]{:S(2)}) copy-start(f32[128,1024]{1,0:T(8,128)} %get-tuple-element.70.sum_in) | copy-start | bytes 1572868
  292.8 4.4 %copy-start.5 = (f32[64,1024]{1,0:T(8,128)S(1)}, f32[64,1024]{1,0:T(8,128)}, u32[]{:S(2)}) copy-start(f32[64,1024]{1,0:T(8,128)} %get-tuple-element.71.sum_out) | copy-start | bytes 786436
  292.8 5.1 %copy-start.14 = (f32[23,64]{1,0:T(8,128)S(1)}, f32[23,64]{1,0:T(8,128)}, u32[]{:S(2)}) copy-start(f32[23,64]{1,0:T(8,128)} %vectors_own.1) | copy-start | bytes 17668
  292.8 5.1 %copy-start.17 = (f32[23,64]{1,0:T(8,128)S(1)}, f32[23,64]{1,0:T(8,128)}, u32[]{:S(2)}) copy-start(f32[23,64]{1,0:T(8,128)} %param.29) | copy-start | bytes 17668
  292.8 5.1 %copy-start.18 = (f32[23,64]{1,0:T(8,128)S(1)}, f32[23,64]{1,0:T(8,128)}, u32[]{:S(2)}) copy-start(f32[23,64]{1,0:T(8,128)} %param.30) | copy-start | bytes 17668
  292.8 5.1 %copy-start.19 = (f32[23,64]{1,0:T(8,128)S(1)}, f32[23,64]{1,0:T(8,128)}, u32[]{:S(2)}) copy-start(f32[23,64]{1,0:T(8,128)} %get-tuple-element.76) | copy-start | bytes 17668
  292.8 5.7 %copy-start.8 = (f32[256,1024]{1,0:T(8,128)S(1)}, f32[256,1024]{1,0:T(8,128)}, u32[]{:S(2)}) copy-start(f32[256,1024]{1,0:T(8,128)} %get-tuple-element.69) | copy-start | bytes 3145732

commit v4 on v2

--- a/solution.py
+++ b/solution.py
@@ -86,6 +86,7 @@
     pre_s,
     dg_s,
     delta_s,
+    sig_s,
     dec_s,
     drive_s,
     dstate_s,
@@ -119,14 +120,19 @@
         keep = masks_ref[pl.ds(r, rows), 1:2] > 0.0
         for j in range(SUBS):
             at = (pl.ds(r, rows), lane_tile(j))
-            delta = jax.nn.softplus(pre_s[at])
+            pre = pre_s[at]
+            z = jnp.exp(-jnp.abs(pre))
+            tail = jnp.where(z < 2.0**-10, z * (1.0 - 0.5 * z), jnp.log(1.0 + z))
+            delta = jnp.maximum(pre, 0.0) + tail
             u = u_ref[at].astype(jnp.float32)
             gate = gate_ref[at]
             delta_s[at] = delta
             to = (pl.ds(r * SUBS + j, rows, stride=SUBS), slice(None))
             dec_s[to] = jnp.where(keep, delta, RESET)
             drive_s[to] = delta * u
-            dstate_s[to] = dg_s[at] * (gate * jax.nn.sigmoid(gate))
+            sig = jax.nn.sigmoid(gate)
+            sig_s[at] = sig
+            dstate_s[to] = dg_s[at] * (gate * sig)
         return carry
 
     lax.fori_loop(0, length // rows, prepare, 0)
@@ -252,7 +258,7 @@
             skip = vec_ref[SKIP : SKIP + 1, j * LANES : (j + 1) * LANES]
             u = u_ref[at].astype(jnp.float32)
             gate = gate_ref[at]
-            sig = jax.nn.sigmoid(gate)
+            sig = sig_s[at]
             act = gate * sig
             dg = dg_s[at]
             y = y_s[of] + skip * u
@@ -332,7 +338,7 @@
             pltpu.VMEM((DSTATE * SUBS, LANES), f32),
             pltpu.VMEM((DSTATE * SUBS, LANES), f32),
         ]
-        + [pltpu.VMEM((length, PASS), f32)] * 3
+        + [pltpu.VMEM((length, PASS), f32)] * 4
         + [pltpu.VMEM((length * SUBS, LANES), f32)] * 6
         + [
             pltpu.VMEM(((length + 1) * DSTATE, SUBS, LANES), f32),

time: 298 us -> 298 us (level)
  no operation moved by 1% of the time
where the time goes in v4:
time: 298 us; the launch traced here: 297 us
  Pallas kernels  285 us (96%)
  other arithmetic  7.28 us (2%)
  local copies, waits for them, and re-layouts  3.77 us (1%)
    pallas_call x1, Pallas kernels, muon_rows(): pl.pallas_call(functools.partial(muon_kernel, fsdp, ns, starts), in_specs...  76.1 us
    pallas_call x1, Pallas kernels, back_and_scatter(): pl.pallas_call(functools.partial(back_kernel, fsdp, ns, per_device), in_s...  75.6 us
    pallas_call x1, Pallas kernels, gather_and_front(): pl.pallas_call(functools.partial(front_kernel, fsdp, ns, per_device, gain...  73.9 us
    pallas_call x1, Pallas kernels, scan_both(): pl.pallas_call(scan_kernel, grid=(inner // PASS,), in_specs=[pl.BlockSpec...  59.4 us

profile of v4, /device:TPU:0, one launch (start us, length us, event | category | flops | bytes accessed | tf_op | source)
XLA Modules:
  0.0 296.9 jit_solution(12720149034254530424)
XLA Ops:
  0.6 73.9 %shard_map.288 = (bf16[32,128,1024]{2,1,0:T(8,128)(2,1)}, bf16[32,64,1024]{2,1,0:T(8,128)(2,1)}, bf16[2048,128]{1,0:T(8,128)(2,1)}, bf16[2048,128]{1,0:T(8,128)(...) custom-call(s32[1,4]{1,0:T(1,128)} %lengths_ref.1, ...), custom_call_target="tpu_custom_call" | custom-call | tf_op jit(solution)/shard_map/pallas_call | solution.py:856
  74.6 59.4 %shard_map.289 = (bf16[256,2048]{1,0:T(8,128)(2,1)}, f32[256,2048]{1,0:T(8,128)}, bf16[256,2048]{1,0:T(8,128)(2,1)}, f32[16,2048]{1,0:T(8,128)}, f32[16,2048]{1,...) custom-call(f32[256,128]{1,0:T(8,128)} %get-tuple-element.47.bc_ref.proj_ref, ...), custom_call_target="tpu_custom_call" | custom-call | flops 201326592 | bytes 12582912 | tf_op jit(solution)/shard_map/pallas_call | solution.py:301
  133.9 0.0 copy-start.15
  134.0 0.0 copy-start.16
  134.0 0.0 copy-start
  134.0 0.0 copy-start.3
  134.0 0.0 copy-start.7
  134.0 75.6 %shard_map.290 = (f32[256,1024]{1,0:T(8,128)}, f32[16,128]{1,0:T(8,128)}, f32[128,1024]{1,0:T(8,128)}, f32[64,1024]{1,0:T(8,128)}, f32[64,256]{1,0:T(8,128)}, /*index=5*/f32[23,64]{1,0:T(8,128)}) custom-call(bf16[32,64,1024]{2,1,0:T(8,128)(2,1)} %bitcast.22, bf16[256,2048]{1,0:T(8,128)(2,1)} %get-tuple-element.56.far_1_, ...), custom_call_target="tpu_custom_call" | custom-call | tf_op jit(solution)/shard_map/pallas_call | solution.py:1282
  209.6 0.0 copy-start.9
  209.6 0.0 copy-start.10
  209.6 0.0 copy-start.11
  209.6 0.0 copy-done.15
  209.6 0.8 slice_add_fusion
  210.4 0.0 copy-done.16
  210.5 0.0 copy-start.12
  210.5 0.0 copy-start.20
  210.5 0.0 copy-start.21
  210.5 0.0 copy-start.22
  210.5 0.8 slice_add_fusion.1
  211.3 0.0 copy-done
  211.3 0.0 copy-done.3
  211.3 0.0 copy-start.1
  211.4 1.0 copy-done.1
  212.4 0.9 copy-done.4
  213.3 0.7 copy-done.6
  214.0 76.1 %shard_map.291 = (bf16[2,128,1024]{2,1,0:T(8,128)(2,1)S(1)}, bf16[2,64,128]{2,1,0:T(8,128)(2,1)S(1)}, f32[16,128]{1,0:T(8,128)S(1)}) custom-call(f32[128,1024]{1,0:T(8,128)S(1)} %copy-done.1, f32[64,1024]{1,0:T(8,128)S(1)} %copy-done.4, f32[128,1024]{1,0:T(8,128)S(1)} %copy-done, f32[64,1024]{1,0:T(8,128)S(1)} %copy-done.3, ...), custom_call_target="tpu_custom_call" | custom-call | tf_op jit(solution)/shard_map/pallas_call | solution.py:1621
  290.1 0.0 copy-start.5
  290.1 0.0 copy-done.7
  290.1 0.0 copy-start.14
  290.1 0.0 copy-start.17
  290.2 0.0 copy-start.18
  290.2 0.0 copy-start.19
  290.2 0.0 copy-start.8
  290.2 0.9 convert_subtract_fusion
  291.1 0.7 bitcast_subtract_fusion
  291.8 0.0 copy-done.10
  291.8 0.6 bitcast_subtract_fusion.1
  292.4 0.6 bitcast_subtract_fusion.2
  293.1 0.0 copy-done.22
  293.1 0.6 divide_subtract_fusion.1
  293.7 0.9 multiply_add_fusion
  294.5 0.0 copy-done.5
  294.5 0.7 multiply_add_fusion.1
  295.3 0.0 copy-done.17
  295.3 0.0 copy-done.19
  295.3 0.6 divide_subtract_fusion
  295.9 0.0 copy-done.8
  295.9 1.0 copy.34
  (15 shorter events, 0.0 us)
Async XLA Ops:
  133.9 75.7 %copy-start.15 = (f32[64,64]{1,0:T(8,128)S(1)}, f32[64,64]{1,0:T(8,128)}, u32[]{:S(2)}) copy-start(f32[64,64]{1,0:T(8,128)} %param.26) | copy-start | bytes 49156
  134.0 76.5 %copy-start.16 = (f32[64,96]{1,0:T(8,128)S(1)}, f32[64,96]{1,0:T(8,128)}, u32[]{:S(2)}) copy-start(f32[64,96]{1,0:T(8,128)} %param.25) | copy-start | bytes 73732
  134.0 77.4 %copy-start = (f32[128,1024]{1,0:T(8,128)S(1)}, f32[128,1024]{1,0:T(8,128)}, u32[]{:S(2)}) copy-start(f32[128,1024]{1,0:T(8,128)} %in_moment.1) | copy-start | bytes 1572868
  134.0 77.3 %copy-start.3 = (f32[64,1024]{1,0:T(8,128)S(1)}, f32[64,1024]{1,0:T(8,128)}, u32[]{:S(2)}) copy-start(f32[64,1024]{1,0:T(8,128)} %out_moment.1) | copy-start | bytes 786436
  134.0 156.1 %copy-start.7 = (f32[128,1024]{1,0:T(8,128)S(1)}, f32[128,1024]{1,0:T(8,128)}, u32[]{:S(2)}) copy-start(f32[128,1024]{1,0:T(8,128)} %in_ref.1) | copy-start | bytes 1572868
  209.6 81.5 %copy-start.9 = (f32[64,1024]{1,0:T(8,128)S(1)}, f32[64,1024]{1,0:T(8,128)}, u32[]{:S(2)}) copy-start(f32[64,1024]{1,0:T(8,128)} %out_ref.1) | copy-start | bytes 786436
  209.6 82.2 %copy-start.10 = (f32[64,64]{1,0:T(8,128)S(1)}, f32[64,64]{1,0:T(8,128)}, u32[]{:S(2)}) copy-start(f32[64,64]{1,0:T(8,128)} %dt_own.1) | copy-start | bytes 49156
  209.6 82.8 %copy-start.11 = (f32[64,96]{1,0:T(8,128)S(1)}, f32[64,96]{1,0:T(8,128)}, u32[]{:S(2)}) copy-start(f32[64,96]{1,0:T(8,128)} %x_own.1) | copy-start | bytes 73732
  210.5 84.1 %copy-start.12 = (f32[64,64]{1,0:T(8,128)}, f32[64,64]{1,0:T(8,128)S(1)}, u32[]{:S(2)}) copy-start(f32[64,64]{1,0:T(8,128)S(1)} %slice_add_fusion) | copy-start | bytes 49156
  210.5 82.6 %copy-start.20 = (f32[32]{0:T(128)S(1)}, f32[32]{0:T(128)}, u32[]{:S(2)}) copy-start(f32[32]{0:T(128)} %param.31) | copy-start | bytes 388
  210.5 82.6 %copy-start.21 = (f32[32]{0:T(128)S(1)}, f32[32]{0:T(128)}, u32[]{:S(2)}) copy-start(f32[32]{0:T(128)} %param.32) | copy-start | bytes 388
  210.5 82.6 %copy-start.22 = (f32[32]{0:T(128)S(1)}, f32[32]{0:T(128)}, u32[]{:S(2)}) copy-start(f32[32]{0:T(128)} %param.33) | copy-start | bytes 388
  211.3 83.2 %copy-start.13 = (f32[64,96]{1,0:T(8,128)}, f32[64,96]{1,0:T(8,128)S(1)}, u32[]{:S(2)}) copy-start(f32[64,96]{1,0:T(8,128)S(1)} %slice_add_fusion.1) | copy-start | bytes 73732
  211.3 1.0 copy-start.1
  212.4 0.9 copy-start.4
  213.3 0.7 copy-start.6
  214.0 79.6 %copy-start.2 = (f32[128,1024]{1,0:T(8,128)S(1)}, f32[128,1024]{1,0:T(8,128)}, u32[]{:S(2)}) copy-start(f32[128,1024]{1,0:T(8,128)} %get-tuple-element.70.sum_in) | copy-start | bytes 1572868
  290.1 4.4 %copy-start.5 = (f32[64,1024]{1,0:T(8,128)S(1)}, f32[64,1024]{1,0:T(8,128)}, u32[]{:S(2)}) copy-start(f32[64,1024]{1,0:T(8,128)} %get-tuple-element.71.sum_out) | copy-start | bytes 786436
  290.1 5.1 %copy-start.14 = (f32[23,64]{1,0:T(8,128)S(1)}, f32[23,64]{1,0:T(8,128)}, u32[]{:S(2)}) copy-start(f32[23,64]{1,0:T(8,128)} %vectors_own.1) | copy-start | bytes 17668
  290.1 5.1 %copy-start.17 = (f32[23,64]{1,0:T(8,128)S(1)}, f32[23,64]{1,0:T(8,128)}, u32[]{:S(2)}) copy-start(f32[23,64]{1,0:T(8,128)} %param.29) | copy-start | bytes 17668
  290.2 5.1 %copy-start.18 = (f32[23,64]{1,0:T(8,128)S(1)}, f32[23,64]{1,0:T(8,128)}, u32[]{:S(2)}) copy-start(f32[23,64]{1,0:T(8,128)} %param.30) | copy-start | bytes 17668
  290.2 5.1 %copy-start.19 = (f32[23,64]{1,0:T(8,128)S(1)}, f32[23,64]{1,0:T(8,128)}, u32[]{:S(2)}) copy-start(f32[23,64]{1,0:T(8,128)} %get-tuple-element.76) | copy-start | bytes 17668
  290.2 5.7 %copy-start.8 = (f32[256,1024]{1,0:T(8,128)S(1)}, f32[256,1024]{1,0:T(8,128)}, u32[]{:S(2)}) copy-start(f32[256,1024]{1,0:T(8,128)} %get-tuple-element.69) | copy-start | bytes 3145732
